TPU v7x, 256 devices: a whole 4x4x8 slice. The times are simulated.
256 devices in a mesh: group: 8 (over y_lo, x), tile: 32 (over z, y_hi, core).
Axes of the slice: x: 4, y: 4 (y_hi: 2, y_lo: 2; y = y_hi * 2 + y_lo), z: 8, core: 2. Of those that a mesh axis runs over, the one named last changes fastest.
Arguments:
- state_in: bfloat16 [256, 200, 8, 128], P(('group', 'tile')), may hold values from -6 to 6
- cotangent: bfloat16 [256, 200, 8, 128], P(('group', 'tile')), may hold values from -6 to 6
- ocean_mask: int32 [256, 8, 128], P(('group', 'tile')), may hold values from 0 to 1, as said below
- slot_column: int32 [256], P(('group', 'tile')), may hold values from -1 to 0, as said below
- dw_taps: bfloat16 [200, 49], replicated, may hold values from -0.875 to 0.875
- dw_bias: bfloat16 [200], replicated, may hold values from -3 to 3
- norm_gain: bfloat16 [200], replicated, may hold values from 0.099609375 to 1.8984375
- norm_bias: bfloat16 [200], replicated, may hold values from -3 to 3
- up_weight: bfloat16 [800, 200], replicated, may hold values from -0.4375 to 0.4375
- up_bias: bfloat16 [800], replicated, may hold values from -3 to 3
- down_weight: bfloat16 [200, 800], replicated, may hold values from -0.21875 to 0.21875
- down_bias: bfloat16 [200], replicated, may hold values from -3 to 3
- layer_scale: bfloat16 [200], replicated, may hold values from 0.5 to 1.5
Outputs:
- grad_state: bfloat16 [256, 200, 8, 128], P(('group', 'tile'))
- grad_up: float32 [800, 200], P('tile')
- grad_up_bias: float32 [800], P('tile')
- grad_down: float32 [200, 800], P(None, 'tile')
- grad_taps: float32 [200, 49], replicated
- grad_vectors: float32 [5, 200], replicated
Inputs may be any that keep to these rules, and one draw needn't show every extreme that they name: `slot_column`: on each device the slots hold, in increasing order, the columns of its block of 1 tile columns that carry ocean, then -1; a device may hold no tile, and in every band some device holds all 1. `ocean_mask`: all zero in slots whose column is -1.
All inputs are finite; a program needn't handle non-finite values.
Results may differ from a plain program's by a relative error of at most 0.0075.
Values may be sent and summed in bfloat16 or wider, within the bound.
A program may use at most 64 MiB of HBM per device.

v0:
```python
import math

import jax
import jax.numpy as jnp
from jax import lax
from jax.sharding import PartitionSpec as P

KERNEL = 7


NORM_EPSILON = 1e-06
SQRT_HALF = 0.7071067811865476
GAUSS_SCALE = 0.3989422804014327


def from_behind(block, axis, distance):
    devices = range(lax.axis_size(axis))
    route = [(i - distance, i) for i in devices if i - distance in devices]
    return lax.ppermute(block, axis, route)


def shifted(block, axis, distance):
    devices = range(lax.axis_size(axis))
    route = [((i - distance) % len(devices), i) for i in devices]
    return lax.ppermute(block, axis, route)


def gelu_parts(values):
    lower_mass = 0.5 * (1.0 + lax.erf(values * SQRT_HALF))
    density = GAUSS_SCALE * jnp.exp(-0.5 * values * values)
    return (values * lower_mass, lower_mass + values * density)


def depthwise(extended, dw_taps, flipped):
    height = extended.shape[1] - KERNEL + 1
    breadth = extended.shape[2] - KERNEL + 1
    source = extended.astype(jnp.float32)
    taps_wide = dw_taps.astype(jnp.float32)
    summed = jnp.zeros((extended.shape[0], height, breadth), jnp.float32)
    for row_tap in range(KERNEL):
        for col_tap in range(KERNEL):
            row_start = KERNEL - 1 - row_tap if flipped else row_tap
            col_start = KERNEL - 1 - col_tap if flipped else col_tap
            weight = taps_wide[:, row_tap * KERNEL + col_tap][:, None, None]
            summed = (
                summed
                + weight
                * source[:, row_start : row_start + height, col_start : col_start + breadth]
            )
    return summed


def tap_grads(extended, own_grad):
    height = own_grad.shape[1]
    breadth = own_grad.shape[2]
    source = extended.astype(jnp.float32)
    columns = []
    for row_tap in range(KERNEL):
        for col_tap in range(KERNEL):
            columns.append(
                jnp.sum(
                    own_grad * source[:, row_tap : row_tap + height, col_tap : col_tap + breadth],
                    axis=(1, 2),
                )
            )
    return jnp.stack(columns, axis=1)


def slot_forward_backward(
    extended,
    mask_cells,
    upstream,
    dw_taps,
    dw_bias,
    norm_gain,
    norm_bias,
    up_weight,
    up_bias,
    down_weight,
    down_bias,
    layer_scale,
):
    channel_count = extended.shape[0]
    conv_out = depthwise(extended, dw_taps, False) + dw_bias.astype(jnp.float32)[:, None, None]
    height = conv_out.shape[1]
    breadth = conv_out.shape[2]
    cell_count = height * breadth
    conv_low = conv_out.astype(jnp.bfloat16).reshape(channel_count, cell_count)
    conv_wide = conv_low.astype(jnp.float32)
    center = jnp.mean(conv_wide, axis=0, keepdims=True)
    offset = conv_wide - center
    spread = lax.rsqrt(jnp.mean(offset * offset, axis=0, keepdims=True) + NORM_EPSILON)
    normed = offset * spread
    gain_col = norm_gain.astype(jnp.float32)[:, None]
    normed_low = (normed * gain_col + norm_bias.astype(jnp.float32)[:, None]).astype(jnp.bfloat16)
    hidden_pre = (
        jnp.dot(up_weight, normed_low, preferred_element_type=jnp.float32)
        + up_bias.astype(jnp.float32)[:, None]
    )
    activated, derivative = gelu_parts(hidden_pre)
    activated_low = activated.astype(jnp.bfloat16)
    branch = (
        jnp.dot(down_weight, activated_low, preferred_element_type=jnp.float32)
        + down_bias.astype(jnp.float32)[:, None]
    )
    mask_row = mask_cells.astype(jnp.float32).reshape(1, cell_count)
    masked_grad = upstream.astype(jnp.float32).reshape(channel_count, cell_count) * mask_row
    grad_scale = jnp.sum(masked_grad * branch, axis=1)
    grad_branch = layer_scale.astype(jnp.float32)[:, None] * masked_grad
    grad_branch_low = grad_branch.astype(jnp.bfloat16)
    grad_down_bias = jnp.sum(grad_branch, axis=1)
    grad_down = lax.dot_general(
        grad_branch_low, activated_low, (((1,), (1,)), ((), ())), preferred_element_type=jnp.float32
    )
    grad_act = lax.dot_general(
        down_weight, grad_branch_low, (((0,), (0,)), ((), ())), preferred_element_type=jnp.float32
    )
    grad_pre = grad_act * derivative
    grad_pre_low = grad_pre.astype(jnp.bfloat16)
    grad_up_bias = jnp.sum(grad_pre, axis=1)
    grad_up = lax.dot_general(
        grad_pre_low, normed_low, (((1,), (1,)), ((), ())), preferred_element_type=jnp.float32
    )
    grad_normed = lax.dot_general(
        up_weight, grad_pre_low, (((0,), (0,)), ((), ())), preferred_element_type=jnp.float32
    )
    grad_gain = jnp.sum(grad_normed * normed, axis=1)
    grad_shift = jnp.sum(grad_normed, axis=1)
    scaled = grad_normed * gain_col
    grad_conv = spread * (
        scaled
        - jnp.mean(scaled, axis=0, keepdims=True)
        - normed * jnp.mean(scaled * normed, axis=0, keepdims=True)
    )
    grad_conv_low = grad_conv.astype(jnp.bfloat16).reshape(channel_count, height, breadth)
    return (
        grad_conv_low,
        (grad_up, grad_up_bias, grad_down, grad_down_bias, grad_scale, grad_gain, grad_shift),
    )


def slot_finish(grad_extended, extended, mask_cells, upstream, dw_taps):
    margin = KERNEL // 2
    height = mask_cells.shape[0]
    breadth = mask_cells.shape[1]
    conv_part = depthwise(grad_extended, dw_taps, True)
    mask_wide = mask_cells.astype(jnp.float32)[None]
    direct = upstream.astype(jnp.float32) * mask_wide
    grad_in = (mask_wide * (direct + conv_part)).astype(jnp.bfloat16)
    own_grad = grad_extended[:, margin : margin + height, margin : margin + breadth].astype(
        jnp.float32
    )
    return (grad_in, tap_grads(extended, own_grad), jnp.sum(own_grad, axis=(1, 2)))


def surround(slot_field, placing):
    margin = KERNEL // 2
    height = slot_field.shape[2]
    by_column = jnp.einsum(
        "sk,schw->kchw", placing, slot_field, preferred_element_type=jnp.float32
    ).astype(jnp.bfloat16)
    from_below = from_behind(by_column[:, :, height - margin :, :], "group", 1)
    from_above = from_behind(by_column[:, :, :margin, :], "group", -1)
    tall_block = jnp.concatenate([from_below, by_column, from_above], axis=2)
    from_west = shifted(tall_block[-1, :, :, -margin:], "tile", 1)
    from_east = shifted(tall_block[0, :, :, :margin], "tile", -1)
    left_part = jnp.concatenate([from_west[None], tall_block[:-1, :, :, -margin:]], axis=0)
    right_part = jnp.concatenate([tall_block[1:, :, :, :margin], from_east[None]], axis=0)
    wide_block = jnp.concatenate([left_part, tall_block, right_part], axis=3)
    return jnp.einsum(
        "sk,kchw->schw", placing, wide_block, preferred_element_type=jnp.float32
    ).astype(jnp.bfloat16)


def local(
    state_in,
    cotangent,
    ocean_mask,
    slot_column,
    dw_taps,
    dw_bias,
    norm_gain,
    norm_bias,
    up_weight,
    up_bias,
    down_weight,
    down_bias,
    layer_scale,
):
    slot_count = state_in.shape[0]
    height = state_in.shape[2]
    breadth = state_in.shape[3]
    placing = (slot_column[:, None] == jnp.arange(slot_count, dtype=jnp.int32)[None, :]).astype(
        jnp.bfloat16
    )
    masked_state = state_in * ocean_mask.astype(jnp.bfloat16)[:, None]
    extended = surround(masked_state, placing)

    def run_slot(slot_items):
        return slot_forward_backward(
            slot_items[0],
            slot_items[1],
            slot_items[2],
            dw_taps,
            dw_bias,
            norm_gain,
            norm_bias,
            up_weight,
            up_bias,
            down_weight,
            down_bias,
            layer_scale,
        )

    grad_conv, stacked = lax.map(run_slot, (extended, ocean_mask, cotangent))
    partials = jax.tree.map(lambda stack_part: jnp.sum(stack_part, axis=0), stacked)
    grad_up, grad_up_bias, grad_down, grad_down_bias, grad_scale, grad_gain, grad_shift = partials
    grad_extended = surround(grad_conv, placing)

    def finish_slot(slot_items):
        return slot_finish(slot_items[0], slot_items[1], slot_items[2], slot_items[3], dw_taps)

    grad_state, taps_stack, bias_stack = lax.map(
        finish_slot, (grad_extended, extended, ocean_mask, cotangent)
    )
    taps_sum = jnp.sum(taps_stack, axis=0)
    bias_sum = jnp.sum(bias_stack, axis=0)
    vectors = jnp.stack([bias_sum, grad_gain, grad_shift, grad_down_bias, grad_scale], axis=0)
    factor = 1.0 / math.sqrt(
        slot_count * height * breadth * lax.axis_size("group") * lax.axis_size("tile")
    )
    totals = lax.psum((grad_up, grad_up_bias, grad_down, taps_sum, vectors), ("group", "tile"))
    share_rows = grad_up.shape[0] // lax.axis_size("tile")
    first_row = lax.axis_index("tile") * share_rows
    up_share = lax.dynamic_slice_in_dim(totals[0], first_row, share_rows, 0)
    up_bias_share = lax.dynamic_slice_in_dim(totals[1], first_row, share_rows, 0)
    down_share = lax.dynamic_slice_in_dim(totals[2], first_row, share_rows, 1)
    taps_total = totals[3]
    vector_total = totals[4]
    return (
        grad_state,
        up_share * factor,
        up_bias_share * factor,
        down_share * factor,
        taps_total * factor,
        vector_total * factor,
    )


def solution(mesh):
    in_specs = (
        P(("group", "tile"), None, None, None),
        P(("group", "tile"), None, None, None),
        P(("group", "tile"), None, None),
        P(("group", "tile")),
        P(),
        P(),
        P(),
        P(),
        P(),
        P(),
        P(),
        P(),
        P(),
    )
    out_specs = (
        P(("group", "tile"), None, None, None),
        P("tile", None),
        P("tile"),
        P(None, "tile"),
        P(),
        P(),
    )
    return jax.shard_map(local, mesh=mesh, in_specs=in_specs, out_specs=out_specs, check_vma=False)
```

profile of v0, /device:TPU:1, one launch (start us, length us, event | category | flops | bytes accessed | tf_op | source)
XLA Modules:
  0.0 359.5 jit_solution(12517140311744163205)
XLA Ops:
  8.9 1.5 copy.58
  10.9 4.1 %collective-permute-start = (bf16[1,200,3,128]{1,2,3,0:T(4,128)(2,1)S(1)}, bf16[1,200,3,128]{1,2,3,0:T(4,128)(2,1)S(1)}, u32[]{:S(2)}, u32[]{:S(2)}) collective-permute-start(bf16[1,200,3,128]{1,2,3,0:T(4,128)(2,1)S(1)} %get-tuple-element.192), channel_id=1, source_target_pairs={{0,32},{32,64},{64,96},{96,128},{128,160},{160,192},{192,224},{1,3... | collective-permute-start | bytes 460808 | tf_op jit(solution)/shard_map/ppermute | solution.py:19
  15.0 1.3 collective-permute-start.1
  19.9 3.8 %collective-permute-done.1 = bf16[1,200,3,128]{1,2,3,0:T(4,128)(2,1)S(1)} collective-permute-done((bf16[1,200,3,128]{1,2,3,0:T(4,128)(2,1)S(1)}, bf16[1,200,3,128]{1,2,3,0:T(4,128)(2,1)S(1)}, u32[]{:S(2)}, u32[]{:S(2)}) %collective-permute-start.1) | collective-permute-done | bytes 153632 | tf_op jit(solution)/shard_map/ppermute | solution.py:19
  23.8 4.7 %collective-permute-start.2 = (bf16[200,14,3]{0,1,2:T(8,128)(2,1)S(1)}, bf16[200,14,3]{0,1,2:T(8,128)(2,1)S(1)}, u32[]{:S(2)}, u32[]{:S(2)}) collective-permute-start(bf16[200,14,3]{0,1,2:T(8,128)(2,1)S(1)} %get-tuple-element.188), channel_id=1, source_target_pairs={{31,0},{0,1},{1,2},{2,3},{3,4},{4,5},{5,6},{6,7},{7,8},{8,9},{9,10... | collective-permute-start | bytes 50408 | tf_op jit(solution)/shard_map/ppermute | solution.py:25
  29.3 1.4 copy.62
  33.6 1.7 fusion.13
  35.4 10.6 %convert_reduce_fusion.1 = (f32[8,128]{0,1:T(8,128)S(1)}, bf16[200,8,128]{0,1,2:T(8,128)(2,1)}) fusion(f32[200]{0:T(256)S(1)} %copy-done.67, f32[200,14,134]{0,1,2:T(8,128)S(1)} %fusion.13, f32[200]{0:T(256)} %bitcast.330, f32[200]{0:T(256)} %bitcast.328, f32[200]{0:T(256)} %bitcast.326, f32[200]{0:T(256)} %bitcast.324, f32[200]{0:T(256)} %bitcast.322, ...), kind=kLoop, calls=%fused_computation.241 | loop fusion | flops 20683776 | bytes 40594496 | tf_op jit(solution)/shard_map/while/body/eval_jaxpr/reduce_sum | solution.py:90
  46.2 2.4 copy.63
  48.6 1.4 multiply_reduce_fusion.1
  50.2 3.6 fusion.8
  53.8 2.7 fusion.136
  56.5 1.6 fusion.117
  58.1 1.4 fusion.116
  60.7 1.3 copy.64
  62.0 2.2 fusion.131
  64.2 3.1 collective-permute-start.4
  67.4 1.3 collective-permute-start.5
  68.7 3.3 fusion.127
  72.0 2.8 collective-permute-done.5
  75.6 5.7 %collective-permute-start.6 = (bf16[200,14,3]{0,1,2:T(8,128)(2,1)S(1)}, bf16[200,14,3]{0,1,2:T(8,128)(2,1)S(1)}, u32[]{:S(2)}, u32[]{:S(2)}) collective-permute-start(bf16[200,14,3]{0,1,2:T(8,128)(2,1)S(1)} %get-tuple-element.186), channel_id=1, source_target_pairs={{31,0},{0,1},{1,2},{2,3},{3,4},{4,5},{5,6},{6,7},{7,8},{8,9},{9,10... | collective-permute-start | bytes 50408 | tf_op jit(solution)/shard_map/ppermute | solution.py:25
  81.5 2.5 fusion.11
  84.0 1.3 reduce_sum.682
  86.0 1.8 fusion.129
  87.9 1.2 fusion.36
  91.6 2.2 fusion.63
  94.2 8.8 %fusion.122 = bf16[1,200,8,128]{1,2,3,0:T(8,128)(2,1)} fusion(f32[200,14,134]{0,1,2:T(8,128)S(1)} %get-tuple-element.178, f32[200]{0:T(256)} %bitcast.331, f32[200]{0:T(256)} %bitcast.329, f32[200]{0:T(256)} %bitcast.327, f32[200]{0:T(256)} %bitcast.325, f32[200]{0:T(256)} %bitcast.323, f32[200]{0:T(256)} %bitcast.321, f32[200]{0:T(256)} %bitcast.319, ...), kind=kLoop, calls=%fused_computation.242 | loop fusion | flops 20889600 | bytes 41003296 | tf_op jit(solution)/shard_map/while/body/jit(dynamic_update_index_in_dim)/broadcast_in_dim | solution.py:215
  104.1 1.3 copy.68
  106.2 84.1 %all-reduce = (f32[800]{0:T(1024)S(1)}, f32[200,49]{0,1:T(8,128)S(1)}, f32[5,200]{1,0:T(8,128)S(1)}) all-reduce(f32[800]{0:T(1024)} %get-tuple-element.251, f32[200,49]{0,1:T(8,128)S(1)} %stack.257, f32[5,200]{1,0:T(8,128)S(1)} %stack.258), channel_id=1, replica_groups=mesh['group'=8,'tile'=32] {'group','tile'}, use_global_device_ids=true, to_apply=%region_6.7 | all-reduce | flops 11600 | bytes 92800 | tf_op jit(solution)/shard_map/psum | solution.py:232
  192.1 157.7 %all-reduce.4.cloned.1.call-done = (f32[800,200]{1,0:T(8,128)}, f32[200,800]{0,1:T(8,128)}) async-done(((f32[800,200]{1,0:T(8,128)}, f32[200,800]{0,1:T(8,128)}), (f32[800,200]{1,0:T(8,128)}, f32[200,800]{0,1:T(8,128)})) %all-reduce.4.cloned.1.call-update) | async-done | bytes 1280016 | tf_op jit(solution)/shard_map/psum | solution.py:232
  349.8 1.4 dynamic-slice_multiply_fusion.1
  351.2 1.4 dynamic-slice_multiply_fusion
  (196 shorter events, 18.0 us)
Async XLA Ops:
  7.2 42.9 %copy-start = (bf16[800,200]{0,1:T(8,128)(2,1)S(1)}, bf16[800,200]{0,1:T(8,128)(2,1)}, u32[]{:S(2)}) copy-start(bf16[800,200]{0,1:T(8,128)(2,1)} %param.21) | copy-start | bytes 960004
  7.2 10.5 %copy-start.69 = (bf16[200]{0:T(256)(128)(2,1)S(1)}, bf16[200]{0:T(256)(128)(2,1)}, u32[]{:S(2)}) copy-start(bf16[200]{0:T(256)(128)(2,1)} %param.25) | copy-start | bytes 1204
  7.2 10.6 %copy-start.7 = (bf16[1,200,8,128]{3,2,1,0:T(8,128)(2,1)S(1)}, bf16[1,200,8,128]{3,2,1,0:T(8,128)(2,1)}, u32[]{:S(2)}) copy-start(bf16[1,200,8,128]{3,2,1,0:T(8,128)(2,1)} %param.14) | copy-start | bytes 1228804
  7.2 342.6 %all-reduce.4.cloned.1.call-start = ((), (), s32[]{:S(2)}) async-start(), calls=%async_computation | async-start | bytes 3276800 | tf_op jit(solution)/shard_map/psum | solution.py:232
  8.7 45.0 %copy-start.9 = (f32[1024]{0:T(1024)}, f32[1024]{0:T(1024)S(1)}, u32[]{:S(2)}) copy-start(f32[1024]{0:T(1024)S(1)} %get-tuple-element.244) | copy-start | bytes 12292
  10.6 20.0 %copy-start.1 = (bf16[1,200,8,128]{1,2,3,0:T(8,128)(2,1)}, bf16[1,200,8,128]{1,2,3,0:T(8,128)(2,1)S(1)}, u32[]{:S(2)}) copy-start(bf16[1,200,8,128]{1,2,3,0:T(8,128)(2,1)S(1)} %multiply_convert_fusion.2) | copy-start | bytes 1228804
  10.8 19.9 %copy-start.70 = (bf16[200]{0:T(256)(128)(2,1)S(1)}, bf16[200]{0:T(256)(128)(2,1)}, u32[]{:S(2)}) copy-start(bf16[200]{0:T(256)(128)(2,1)} %param.19) | copy-start | bytes 1204
  10.8 20.4 %copy-start.71 = (bf16[200]{0:T(256)(128)(2,1)S(1)}, bf16[200]{0:T(256)(128)(2,1)}, u32[]{:S(2)}) copy-start(bf16[200]{0:T(256)(128)(2,1)} %param.20) | copy-start | bytes 1204
  10.8 20.9 %copy-start.72 = (bf16[200]{0:T(256)(128)(2,1)S(1)}, bf16[200]{0:T(256)(128)(2,1)}, u32[]{:S(2)}) copy-start(bf16[200]{0:T(256)(128)(2,1)} %param.18) | copy-start | bytes 1204
  10.8 21.4 %copy-start.73 = (bf16[200]{0:T(256)(128)(2,1)S(1)}, bf16[200]{0:T(256)(128)(2,1)}, u32[]{:S(2)}) copy-start(bf16[200]{0:T(256)(128)(2,1)} %param.24) | copy-start | bytes 1204
  10.9 22.0 %copy-start.65 = (bf16[800]{0:T(1024)(128)(2,1)S(1)}, bf16[800]{0:T(1024)(128)(2,1)}, u32[]{:S(2)}) copy-start(bf16[800]{0:T(1024)(128)(2,1)} %param.22) | copy-start | bytes 4804
  10.9 9.0 %collective-permute-start = (bf16[1,200,3,128]{1,2,3,0:T(4,128)(2,1)S(1)}, bf16[1,200,3,128]{1,2,3,0:T(4,128)(2,1)S(1)}, u32[]{:S(2)}, u32[]{:S(2)}) collective-permute-start(bf16[1,200,3,128]{1,2,3,0:T(4,128)(2,1)S(1)} %get-tuple-element.192), channel_id=1, source_target_pairs={{0,32},{32,64},{64,96},{96,128},{128,160},{160,192},{192,224},{1,3... | collective-permute-start | bytes 460808 | tf_op jit(solution)/shard_map/ppermute | solution.py:19
  15.0 8.8 %collective-permute-start.1 = (bf16[1,200,3,128]{1,2,3,0:T(4,128)(2,1)S(1)}, bf16[1,200,3,128]{1,2,3,0:T(4,128)(2,1)S(1)}, u32[]{:S(2)}, u32[]{:S(2)}) collective-permute-start(bf16[1,200,3,128]{1,2,3,0:T(4,128)(2,1)S(1)} %get-tuple-element.193), channel_id=1, source_target_pairs={{32,0},{64,32},{96,64},{128,96},{160,128},{192,160},{224,192},{33,... | collective-permute-start | bytes 460808 | tf_op jit(solution)/shard_map/ppermute | solution.py:19
  16.9 18.4 %copy-start.11 = (f32[200,1]{0,1:T(1,128)}, f32[200,1]{0,1:T(1,128)S(1)}, u32[]{:S(2)}) copy-start(f32[200,1]{0,1:T(1,128)S(1)} %get-tuple-element.213) | copy-start | bytes 2404
  16.9 18.4 %copy-start.13 = (f32[200,1]{0,1:T(1,128)}, f32[200,1]{0,1:T(1,128)S(1)}, u32[]{:S(2)}) copy-start(f32[200,1]{0,1:T(1,128)S(1)} %get-tuple-element.214) | copy-start | bytes 2404
  16.9 18.4 %copy-start.15 = (f32[200,1]{0,1:T(1,128)}, f32[200,1]{0,1:T(1,128)S(1)}, u32[]{:S(2)}) copy-start(f32[200,1]{0,1:T(1,128)S(1)} %get-tuple-element.215) | copy-start | bytes 2404
  16.9 18.4 %copy-start.17 = (f32[200,1]{0,1:T(1,128)}, f32[200,1]{0,1:T(1,128)S(1)}, u32[]{:S(2)}) copy-start(f32[200,1]{0,1:T(1,128)S(1)} %get-tuple-element.216) | copy-start | bytes 2404
  16.9 18.4 %copy-start.19 = (f32[200,1]{0,1:T(1,128)}, f32[200,1]{0,1:T(1,128)S(1)}, u32[]{:S(2)}) copy-start(f32[200,1]{0,1:T(1,128)S(1)} %get-tuple-element.217) | copy-start | bytes 2404
  16.9 18.4 %copy-start.21 = (f32[200,1]{0,1:T(1,128)}, f32[200,1]{0,1:T(1,128)S(1)}, u32[]{:S(2)}) copy-start(f32[200,1]{0,1:T(1,128)S(1)} %get-tuple-element.218) | copy-start | bytes 2404
  17.0 18.4 %copy-start.23 = (f32[200,1]{0,1:T(1,128)}, f32[200,1]{0,1:T(1,128)S(1)}, u32[]{:S(2)}) copy-start(f32[200,1]{0,1:T(1,128)S(1)} %get-tuple-element.219) | copy-start | bytes 2404
  17.0 18.4 %copy-start.25 = (f32[200,1]{0,1:T(1,128)}, f32[200,1]{0,1:T(1,128)S(1)}, u32[]{:S(2)}) copy-start(f32[200,1]{0,1:T(1,128)S(1)} %get-tuple-element.220) | copy-start | bytes 2404
  17.0 18.4 %copy-start.27 = (f32[200,1]{0,1:T(1,128)}, f32[200,1]{0,1:T(1,128)S(1)}, u32[]{:S(2)}) copy-start(f32[200,1]{0,1:T(1,128)S(1)} %get-tuple-element.221) | copy-start | bytes 2404
  17.0 18.4 %copy-start.29 = (f32[200,1]{0,1:T(1,128)}, f32[200,1]{0,1:T(1,128)S(1)}, u32[]{:S(2)}) copy-start(f32[200,1]{0,1:T(1,128)S(1)} %get-tuple-element.222) | copy-start | bytes 2404
  17.7 15.9 %copy-start.62 = (f32[200]{0:T(256)}, f32[200]{0:T(256)S(1)}, u32[]{:S(2)}) copy-start(f32[200]{0:T(256)S(1)} %convert_element_type.160) | copy-start | bytes 2404
  23.8 9.7 %collective-permute-start.2 = (bf16[200,14,3]{0,1,2:T(8,128)(2,1)S(1)}, bf16[200,14,3]{0,1,2:T(8,128)(2,1)S(1)}, u32[]{:S(2)}, u32[]{:S(2)}) collective-permute-start(bf16[200,14,3]{0,1,2:T(8,128)(2,1)S(1)} %get-tuple-element.188), channel_id=1, source_target_pairs={{31,0},{0,1},{1,2},{2,3},{3,4},{4,5},{5,6},{6,7},{7,8},{8,9},{9,10... | collective-permute-start | bytes 50408 | tf_op jit(solution)/shard_map/ppermute | solution.py:25
  28.5 5.1 %collective-permute-start.3 = (bf16[200,14,3]{0,1,2:T(8,128)(2,1)S(1)}, bf16[200,14,3]{0,1,2:T(8,128)(2,1)S(1)}, u32[]{:S(2)}, u32[]{:S(2)}) collective-permute-start(bf16[200,14,3]{0,1,2:T(8,128)(2,1)S(1)} %get-tuple-element.189), channel_id=1, source_target_pairs={{1,0},{2,1},{3,2},{4,3},{5,4},{6,5},{7,6},{8,7},{9,8},{10,9},{11,1... | collective-permute-start | bytes 50408 | tf_op jit(solution)/shard_map/ppermute | solution.py:25
  64.2 7.8 %collective-permute-start.4 = (bf16[1,200,3,128]{1,2,3,0:T(4,128)(2,1)}, bf16[1,200,3,128]{1,2,3,0:T(4,128)(2,1)S(1)}, u32[]{:S(2)}, u32[]{:S(2)}) collective-permute-start(bf16[1,200,3,128]{1,2,3,0:T(4,128)(2,1)} %get-tuple-element.190), channel_id=1, source_target_pairs={{0,32},{32,64},{64,96},{96,128},{128,160},{160,192},{192,224},{1,3... | collective-permute-start | bytes 460808 | tf_op jit(solution)/shard_map/ppermute | solution.py:19
  67.3 14.2 %copy-start.10 = (f32[1024]{0:T(1024)S(1)}, f32[1024]{0:T(1024)}, u32[]{:S(2)}) copy-start(f32[1024]{0:T(1024)} %copy-done.9) | copy-start | bytes 12292
  67.4 14.2 %copy-start.74 = (f32[200]{0:T(256)S(1)}, f32[200]{0:T(256)}, u32[]{:S(2)}) copy-start(f32[200]{0:T(256)} %convert_element_type.182) | copy-start | bytes 2404
  67.4 7.4 %collective-permute-start.5 = (bf16[1,200,3,128]{1,2,3,0:T(4,128)(2,1)}, bf16[1,200,3,128]{1,2,3,0:T(4,128)(2,1)}, u32[]{:S(2)}, u32[]{:S(2)}) collective-permute-start(bf16[1,200,3,128]{1,2,3,0:T(4,128)(2,1)} %get-tuple-element.191), channel_id=1, source_target_pairs={{32,0},{64,32},{96,64},{128,96},{160,128},{192,160},{224,192},{33,... | collective-permute-start | bytes 460808 | tf_op jit(solution)/shard_map/ppermute | solution.py:19
  75.6 9.7 %collective-permute-start.6 = (bf16[200,14,3]{0,1,2:T(8,128)(2,1)S(1)}, bf16[200,14,3]{0,1,2:T(8,128)(2,1)S(1)}, u32[]{:S(2)}, u32[]{:S(2)}) collective-permute-start(bf16[200,14,3]{0,1,2:T(8,128)(2,1)S(1)} %get-tuple-element.186), channel_id=1, source_target_pairs={{31,0},{0,1},{1,2},{2,3},{3,4},{4,5},{5,6},{6,7},{7,8},{8,9},{9,10... | collective-permute-start | bytes 50408 | tf_op jit(solution)/shard_map/ppermute | solution.py:25
  81.3 4.8 %collective-permute-start.7 = (bf16[200,14,3]{0,1,2:T(8,128)(2,1)S(1)}, bf16[200,14,3]{0,1,2:T(8,128)(2,1)S(1)}, u32[]{:S(2)}, u32[]{:S(2)}) collective-permute-start(bf16[200,14,3]{0,1,2:T(8,128)(2,1)S(1)} %get-tuple-element.187), channel_id=1, source_target_pairs={{1,0},{2,1},{3,2},{4,3},{5,4},{6,5},{7,6},{8,7},{9,8},{10,9},{11,1... | collective-permute-start | bytes 50408 | tf_op jit(solution)/shard_map/ppermute | solution.py:25
  (53 other events, 159.3 us)
Sparse Core Ops, SparseCore 0:
  85.4 264.3 all-reduce.3
where the time goes:
time: 362 us; the launch traced here: 359 us
  waiting for transfers between devices  166 us (46%)
  blocking collectives  84.1 us (23%)
  other arithmetic  42.4 us (12%)
  starting transfers between devices  20.5 us (6%)
  between operations  15.9 us (4%)
  local copies, waits for them, and re-layouts  15.3 us (4%)
  matrix products  15 us (4%)
    psum x1, waiting for transfers between devices, local(): lax.psum((grad_up, grad_up_bias, grad_down, taps_sum, vectors), ('group',...  158 us
    psum x1, blocking collectives, local(): lax.psum((grad_up, grad_up_bias, grad_down, taps_sum, vectors), ('group',...  84.1 us
    ppermute x4, starting transfers between devices, shifted(): return lax.ppermute(block, axis, route)  10.7 us
    reduce_sum x1, other arithmetic, slot_forward_backward(): center = jnp.mean(conv_wide, axis=0, keepdims=True)  10.6 us
    ppermute x4, starting transfers between devices, from_behind(): return lax.ppermute(block, axis, route)  9.78 us
    broadcast_in_dim x1, other arithmetic, local(): grad_conv, stacked = lax.map(run_slot, (extended, ocean_mask, cotangent))  8.78 us
    ppermute x4, waiting for transfers between devices, from_behind(): return lax.ppermute(block, axis, route)  7.59 us
  transfers between devices with their start and end apart: 9, of which 6 were waited for; matrix products, arithmetic and copies ran while one was open for 10% of the time, Pallas kernels for 0%

commit v1 on v0

v1 whole, which is shorter than its diff:
```python
import functools
import math

import jax
import jax.numpy as jnp
from jax import lax
from jax.experimental import pallas as pl
from jax.experimental.pallas import tpu as pltpu
from jax.sharding import PartitionSpec as P

MESH = pl.DeviceIdType.MESH
F32 = jnp.float32
BF16 = jnp.bfloat16

CHANNELS = 200
PADDED = 208
HIDDEN = 800
KERNEL = 7
TAPS = KERNEL * KERNEL
MARGIN = 3
ROWS = 8
COLS = 128
CELLS = ROWS * COLS
TALL = ROWS + 2 * MARGIN
BLOCKS = CHANNELS // 8
FOLD = 104
GROUPS = 8
TILES = 32
CHIPS = TILES // 2
SHARE = HIDDEN // TILES
CHUNK = 80

NORM_EPSILON = 1e-06
SQRT_HALF = 0.7071067811865476
GAUSS_SCALE = 0.3989422804014327

DW_BIAS, GAIN, SHIFT, DOWN_BIAS, SCALE = range(TAPS, TAPS + 5)


def lanes_of(shape):
    return lax.broadcasted_iota(jnp.int32, shape, len(shape) - 1)


def source_row(row):
    if row < MARGIN:
        return 1, row + ROWS - MARGIN
    if row < MARGIN + ROWS:
        return 0, row - MARGIN
    return 2, row - MARGIN - ROWS


def shifted_rows(ext, sides, rows, column):
    move = column - MARGIN
    lane = lanes_of((8, COLS))
    out = []
    for row in range(TALL):
        main = ext[row, rows, :]
        if move > 0:
            main = pltpu.roll(jnp.where(lane < move, sides[row], main), COLS - move, 1)
        elif move < 0:
            main = pltpu.roll(jnp.where(lane >= COLS + move, sides[row], main), -move, 1)
        out.append(main)
    return out


def side_rows(packs, rows):
    out = []
    for row in range(TALL):
        pack, origin = source_row(row)
        turn = (COLS - 8 * origin) % COLS
        side = packs[pack, rows, :]
        out.append(pltpu.roll(side, turn, 1) if turn else side)
    return out


def convolve(ext, packs, taps, rows, flipped, keep=None):
    sides = side_rows(packs, rows)
    total = [None] * ROWS
    for column in range(KERNEL):
        moved = shifted_rows(ext, sides, rows, column)
        if keep is not None:
            for row in range(TALL):
                keep[column, row, rows, :] = moved[row]
        for tap_row in range(KERNEL):
            index = tap_row * KERNEL + column
            weight = taps[TAPS - 1 - index if flipped else index, rows, :]
            for row in range(ROWS):
                term = weight * moved[row + tap_row]
                total[row] = term if total[row] is None else total[row] + term
    return total


def block_rows(block):
    return pl.ds(pl.multiple_of(block * 8, 8), 8)


def lane_slice(row):
    return pl.ds(pl.multiple_of(row * COLS, COLS), COLS)


def kernel(
    slot_ref,
    mask_ref,
    state_ref,
    cot_ref,
    cols_ref,
    upw_ref,
    downw_ref,
    gs_ref,
    tail_ref,
    flat,
    ext,
    exg,
    packs_s,
    packs_g,
    taps,
    kept,
    normed,
    spread,
    mgrad,
    nlow,
    gblow,
    act,
    gpre,
    branch,
    gnorm,
    up_t,
    down_t,
    gup,
    gdown,
    sums,
    small_wide,
    gstate,
    rows_send,
    rows_recv,
    pack_send,
    pack_recv,
    w_send,
    w_core,
    w_group,
    w_group_in,
    small,
    small_core,
    small_group,
    small_group_in,
    tile_send,
    tile_in,
    final,
    halo_ssem,
    halo_rsem,
    core_ssem,
    core_rsem,
    wgroup_ssem,
    wgroup_rsem,
    sgroup_ssem,
    sgroup_rsem,
    tile_ssem,
    tile_rsem,
    final_ssem,
    final_rsem,
):
    g = lax.axis_index("group")
    t = lax.axis_index("tile")
    core = lax.rem(t, 2)
    chip = t // 2
    partner = chip * 2 + 1 - core
    east = lax.rem(t + 1, TILES)
    west = lax.rem(t + TILES - 1, TILES)
    has_above = g > 0
    has_below = g < GROUPS - 1

    barrier = pltpu.get_barrier_semaphore()

    def greet(gg, tt):
        pl.semaphore_signal(barrier, inc=1, device_id=(gg, tt), device_id_type=MESH)

    greet(g, partner)
    greet(g, east)
    greet(g, west)
    for k in range(1, GROUPS):
        greet(lax.rem(g + k, GROUPS), t)
    for k in range(1, CHIPS):
        greet(g, lax.rem(chip + k, CHIPS) * 2 + core)

    @pl.when(has_above)
    def _():
        greet(g - 1, east)
        greet(g - 1, west)

    @pl.when(has_below)
    def _():
        greet(g + 1, east)
        greet(g + 1, west)

    def halo_copies(phase):
        def rows_copy(slot, gg):
            return pltpu.make_async_remote_copy(
                src_ref=rows_send.at[phase, slot],
                dst_ref=rows_recv.at[phase, slot],
                send_sem=halo_ssem.at[phase, slot],
                recv_sem=halo_rsem.at[phase, slot],
                device_id=(gg, t),
                device_id_type=MESH,
            )

        def pack_copy(slot, gg, tt):
            return pltpu.make_async_remote_copy(
                src_ref=pack_send.at[phase],
                dst_ref=pack_recv.at[phase, slot],
                send_sem=halo_ssem.at[phase, 2 + slot],
                recv_sem=halo_rsem.at[phase, 2 + slot],
                device_id=(gg, tt),
                device_id_type=MESH,
            )

        side = [pack_copy(0, g, west), pack_copy(1, g, east)]
        down = [rows_copy(0, g + 1), pack_copy(2, g + 1, west), pack_copy(3, g + 1, east)]
        up = [rows_copy(1, g - 1), pack_copy(4, g - 1, west), pack_copy(5, g - 1, east)]
        return side, down, up

    def halo_start(phase):
        side, down, up = halo_copies(phase)

        @pl.when(has_below)
        def _():
            for copy in down:
                copy.start()

        @pl.when(has_above)
        def _():
            for copy in up:
                copy.start()

        for copy in side:
            copy.start()

    def halo_wait(phase):
        side, down, up = halo_copies(phase)
        for copy in side:
            copy.wait_send()
            copy.wait_recv()

        @pl.when(has_below)
        def _():
            for copy in down:
                copy.wait_send()
            for copy in up:
                copy.wait_recv()

        @pl.when(has_above)
        def _():
            for copy in up:
                copy.wait_send()
            for copy in down:
                copy.wait_recv()

    def pack_up(phase, field):
        lane = lanes_of((CHANNELS, COLS))
        spot = lax.rem(lane + 3, COLS) // 8
        pack = field[MARGIN]
        for row in range(1, ROWS):
            pack = jnp.where(spot == row, pltpu.roll(field[MARGIN + row], 8 * row, 1), pack)
        second = pltpu.roll(pack[FOLD:], 64, 1)
        lane = lanes_of((CHANNELS - FOLD, COLS))
        first = jnp.where((lane >= 61) & (lane < 125), second, pack[: CHANNELS - FOLD])
        zeros = jnp.zeros((8, COLS), F32)
        whole = jnp.concatenate([first, pack[CHANNELS - FOLD : FOLD], zeros], axis=0)
        pack_send[phase] = whole.astype(BF16)
        pad = jnp.zeros((MARGIN, PADDED - CHANNELS, COLS), BF16)
        bottom = field[ROWS : ROWS + MARGIN].astype(BF16)
        top = field[MARGIN : 2 * MARGIN].astype(BF16)
        rows_send[phase, 0] = jnp.concatenate([bottom, pad], axis=1)
        rows_send[phase, 1] = jnp.concatenate([top, pad], axis=1)

    def unpack(phase, field, packs):
        field[:MARGIN] = rows_recv[phase, 0].astype(F32)[:, :CHANNELS]
        field[MARGIN + ROWS :] = rows_recv[phase, 1].astype(F32)[:, :CHANNELS]
        lane = lanes_of((112, COLS))
        for index in range(3):
            from_east = pack_recv[phase, 2 * index].astype(F32)
            from_west = pack_recv[phase, 2 * index + 1].astype(F32)
            both = jnp.where(lax.rem(lane, 8) < 4, from_east, from_west)
            packs[index, :FOLD, :] = both[:FOLD]
            packs[index, FOLD:, :] = pltpu.roll(both[: CHANNELS - FOLD], 64, 1)

    @pl.when(jnp.logical_not(has_above))
    def _():
        for phase in range(2):
            rows_recv[phase, 0] = jnp.zeros((MARGIN, PADDED, COLS), BF16)
            pack_recv[phase, 2] = jnp.zeros((112, COLS), BF16)
            pack_recv[phase, 3] = jnp.zeros((112, COLS), BF16)

    @pl.when(jnp.logical_not(has_below))
    def _():
        for phase in range(2):
            rows_recv[phase, 1] = jnp.zeros((MARGIN, PADDED, COLS), BF16)
            pack_recv[phase, 4] = jnp.zeros((112, COLS), BF16)
            pack_recv[phase, 5] = jnp.zeros((112, COLS), BF16)

    live = (slot_ref[0] >= 0).astype(F32)
    mask = mask_ref[...].astype(F32) * live
    flat[...] = (state_ref[...].astype(F32) * mask[None]).reshape(CHANNELS * ROWS, COLS)
    for row in range(ROWS):
        ext[MARGIN + row] = flat[pl.ds(row, CHANNELS, stride=ROWS), :]
    pack_up(0, ext)
    met = 3 + (GROUPS - 1) + (CHIPS - 1)
    met = met + 2 * has_above.astype(jnp.int32) + 2 * has_below.astype(jnp.int32)
    pl.semaphore_wait(barrier, met)
    halo_start(0)

    flat[...] = (cot_ref[...].astype(F32) * mask[None]).reshape(CHANNELS * ROWS, COLS)
    scale_col = cols_ref[:, SCALE : SCALE + 1]
    for row in range(ROWS):
        masked = flat[pl.ds(row, CHANNELS, stride=ROWS), :]
        mgrad[row] = masked
        gblow[:, row * COLS : (row + 1) * COLS] = (masked * scale_col).astype(BF16)
    for tap in range(TAPS):
        taps[tap] = jnp.broadcast_to(cols_ref[:, tap : tap + 1], (CHANNELS, COLS))
    up_t[...] = upw_ref[...].T
    down_t[...] = downw_ref[...].T

    halo_wait(0)
    unpack(0, ext, packs_s)

    @pl.loop(0, BLOCKS)
    def _(block):
        rows = block_rows(block)
        total = convolve(ext, packs_s, taps, rows, False, kept)
        bias = cols_ref[rows, DW_BIAS : DW_BIAS + 1]
        for row in range(ROWS):
            normed[row, rows, :] = (total[row] * live + bias).astype(BF16).astype(F32)

    gain_col = cols_ref[:, GAIN : GAIN + 1]
    shift_col = cols_ref[:, SHIFT : SHIFT + 1]

    @pl.loop(0, ROWS)
    def _(row):
        conv = normed[row]
        offset = conv - jnp.mean(conv, axis=0, keepdims=True)
        rate = lax.rsqrt(jnp.mean(offset * offset, axis=0, keepdims=True) + NORM_EPSILON)
        unit = offset * rate
        spread[row] = rate
        normed[row] = unit
        low = (unit * gain_col + shift_col).astype(BF16)
        tail = (lax.broadcasted_iota(jnp.int32, (PADDED - CHANNELS, COLS), 0) == 0).astype(BF16)
        nlow[:, lane_slice(row)] = jnp.concatenate([low, tail], axis=0)

    @pl.loop(0, HIDDEN // CHUNK)
    def _(chunk):
        units = pl.ds(pl.multiple_of(chunk * CHUNK, CHUNK), CHUNK)
        pre = jnp.dot(upw_ref[units, :], nlow[...], preferred_element_type=F32)
        mass = 0.5 * (1.0 + lax.erf(pre * SQRT_HALF))
        density = GAUSS_SCALE * jnp.exp(-0.5 * pre * pre)
        act[units, :] = (pre * mass).astype(BF16)
        grad_act = jnp.dot(down_t[units, :], gblow[...], preferred_element_type=F32)
        gpre[units, :] = (grad_act * (mass + pre * density)).astype(BF16)

    branch[...] = jnp.dot(downw_ref[...], act[...], preferred_element_type=F32)
    gnorm[...] = jnp.dot(up_t[...], gpre[...], preferred_element_type=F32)[:CHANNELS]

    sums[...] = jnp.zeros_like(sums)
    down_bias = cols_ref[:, DOWN_BIAS : DOWN_BIAS + 1]

    @pl.loop(0, ROWS)
    def _(row):
        grad = gnorm[:, lane_slice(row)]
        unit = normed[row]
        masked = mgrad[row]
        sums[1] += grad * unit
        sums[2] += grad
        sums[3] += masked * scale_col
        sums[4] += masked * (branch[:, lane_slice(row)] + down_bias)
        scaled = grad * gain_col
        first = jnp.mean(scaled, axis=0, keepdims=True)
        second = jnp.mean(scaled * unit, axis=0, keepdims=True)
        low = (spread[row] * (scaled - first - unit * second)).astype(BF16).astype(F32)
        exg[MARGIN + row] = low
        sums[0] += low

    pack_up(1, exg)
    halo_start(1)

    trans = (((1,), (1,)), ((), ()))
    gup[:HIDDEN, :PADDED] = lax.dot_general(gpre[...], nlow[...], trans, preferred_element_type=F32)
    gdown[:HIDDEN, :CHANNELS] = lax.dot_general(
        act[...], gblow[...], trans, preferred_element_type=F32
    )
    for tile in range(TILES):
        for half in range(2):
            begin = tile * SHARE + 16 * half
            size = 16
            if begin + size > HIDDEN:
                size = HIDDEN - begin
            for part in range(4):
                source = gup if part < 2 else gdown
                side = (part % 2) * COLS
                if size < 16:
                    piece = source[begin : begin + 16, side : side + COLS]
                    keep = lax.broadcasted_iota(jnp.int32, (16, COLS), 0) < size
                    piece = jnp.where(keep, piece, 0.0)
                else:
                    piece = source[begin : begin + 16, side : side + COLS]
                w_send[tile % 2, half * 4 + part, tile // 2] = piece.astype(BF16)

    w_core_copy = pltpu.make_async_remote_copy(
        src_ref=w_send.at[1 - core],
        dst_ref=w_core,
        send_sem=core_ssem.at[0],
        recv_sem=core_rsem.at[0],
        device_id=(g, partner),
        device_id_type=MESH,
    )
    w_core_copy.start()

    def tap_block(block):
        rows = block_rows(block)
        lane = lanes_of((8, COLS))
        own = [exg[MARGIN + row, rows, :] for row in range(ROWS)]
        out = jnp.zeros((8, COLS), F32)
        for column in range(KERNEL):
            moved = [kept[column, row, rows, :] for row in range(TALL)]
            for tap_row in range(KERNEL):
                total = own[0] * moved[tap_row]
                for row in range(1, ROWS):
                    total = total + own[row] * moved[row + tap_row]
                out = jnp.where(
                    lane == tap_row * KERNEL + column, jnp.sum(total, axis=1, keepdims=True), out
                )
        for vector in range(5):
            total = jnp.sum(sums[vector, rows, :], axis=1, keepdims=True)
            out = jnp.where(lane == TAPS + vector, total, out)
        small_wide[rows, :] = out * live

    def finish_block(block):
        rows = block_rows(block)
        total = convolve(exg, packs_g, taps, rows, True)
        for row in range(ROWS):
            cell = mask[row : row + 1]
            gstate[row, rows, :] = cell * (mgrad[row, rows, :] + total[row])

    pl.loop(0, BLOCKS // 2)(tap_block)

    w_core_copy.wait_send()
    w_core_copy.wait_recv()

    @pl.loop(0, GROUPS)
    def _(piece):
        total = w_send[core, piece].astype(F32) + w_core[piece].astype(F32)
        w_group[piece] = total.astype(BF16)

    def w_group_copy(k):
        other = lax.rem(g + k, GROUPS)
        return pltpu.make_async_remote_copy(
            src_ref=w_group.at[other],
            dst_ref=w_group_in.at[k],
            send_sem=wgroup_ssem.at[k],
            recv_sem=wgroup_rsem.at[k],
            device_id=(other, t),
            device_id_type=MESH,
        )

    for k in range(1, GROUPS):
        w_group_copy(k).start()

    pl.loop(BLOCKS // 2, BLOCKS)(tap_block)

    small[:FOLD] = small_wide[:FOLD]
    small[FOLD:] = jnp.zeros((128 - FOLD, COLS), F32)
    small[: CHANNELS - FOLD] += pltpu.roll(small_wide[FOLD:], 64, 1)
    s_core_copy = pltpu.make_async_remote_copy(
        src_ref=small,
        dst_ref=small_core,
        send_sem=core_ssem.at[1],
        recv_sem=core_rsem.at[1],
        device_id=(g, partner),
        device_id_type=MESH,
    )
    s_core_copy.start()

    halo_wait(1)
    unpack(1, exg, packs_g)
    pl.loop(0, BLOCKS // 2)(finish_block)

    s_core_copy.wait_send()
    s_core_copy.wait_recv()
    small_group[...] = (small[...] + small_core[...]).reshape(GROUPS, 16, COLS)

    def s_group_copy(k):
        other = lax.rem(g + k, GROUPS)
        return pltpu.make_async_remote_copy(
            src_ref=small_group.at[other],
            dst_ref=small_group_in.at[k],
            send_sem=sgroup_ssem.at[k],
            recv_sem=sgroup_rsem.at[k],
            device_id=(other, t),
            device_id_type=MESH,
        )

    for k in range(1, GROUPS):
        s_group_copy(k).start()

    pl.loop(BLOCKS // 2, BLOCKS)(finish_block)
    gs_ref[...] = gstate[...].astype(BF16)

    total = w_group[g].astype(F32)
    for k in range(1, GROUPS):
        w_group_copy(k).wait_send()
        w_group_copy(k).wait_recv()
        total = total + w_group_in[k].astype(F32)
    tile_send[:, 0] = total.astype(BF16)
    total = small_group[g]
    for k in range(1, GROUPS):
        s_group_copy(k).wait_send()
        s_group_copy(k).wait_recv()
        total = total + small_group_in[k]
    low = total.astype(BF16)
    for other in range(CHIPS):
        tile_send[other, 1] = low

    def tile_copy(k):
        other = lax.rem(chip + k, CHIPS)
        return pltpu.make_async_remote_copy(
            src_ref=tile_send.at[other],
            dst_ref=tile_in.at[chip],
            send_sem=tile_ssem.at[k],
            recv_sem=tile_rsem.at[k],
            device_id=(g, other * 2 + core),
            device_id_type=MESH,
        )

    for k in range(1, CHIPS):
        tile_copy(k).start()
    tile_in[chip] = tile_send[chip]
    for k in range(1, CHIPS):
        tile_copy(k).wait_send()
        tile_copy(k).wait_recv()
    total = tile_in[0].astype(F32)
    for other in range(1, CHIPS):
        total = total + tile_in[other].astype(F32)
    final[g] = total

    def final_copy(k):
        other = lax.rem(g + k, GROUPS)
        return pltpu.make_async_remote_copy(
            src_ref=final.at[g],
            dst_ref=final.at[g],
            send_sem=final_ssem.at[k],
            recv_sem=final_rsem.at[k],
            device_id=(other, t),
            device_id_type=MESH,
        )

    for k in range(1, GROUPS):
        final_copy(k).start()
    for k in range(1, GROUPS):
        final_copy(k).wait_send()
        final_copy(k).wait_recv()
    tail_ref[...] = final[...] * (1.0 / math.sqrt(CELLS * GROUPS * TILES))


def scratch():
    dma = pltpu.SemaphoreType.DMA
    return [
        pltpu.VMEM((CHANNELS * ROWS, COLS), F32),
        pltpu.VMEM((TALL, CHANNELS, COLS), F32),
        pltpu.VMEM((TALL, CHANNELS, COLS), F32),
        pltpu.VMEM((3, CHANNELS, COLS), F32),
        pltpu.VMEM((3, CHANNELS, COLS), F32),
        pltpu.VMEM((TAPS, CHANNELS, COLS), F32),
        pltpu.VMEM((KERNEL, TALL, CHANNELS, COLS), F32),
        pltpu.VMEM((ROWS, CHANNELS, COLS), F32),
        pltpu.VMEM((ROWS, 1, COLS), F32),
        pltpu.VMEM((ROWS, CHANNELS, COLS), F32),
        pltpu.VMEM((PADDED, CELLS), BF16),
        pltpu.VMEM((CHANNELS, CELLS), BF16),
        pltpu.VMEM((HIDDEN, CELLS), BF16),
        pltpu.VMEM((HIDDEN, CELLS), BF16),
        pltpu.VMEM((CHANNELS, CELLS), F32),
        pltpu.VMEM((CHANNELS, CELLS), F32),
        pltpu.VMEM((PADDED, HIDDEN), BF16),
        pltpu.VMEM((HIDDEN, CHANNELS), BF16),
        pltpu.VMEM((HIDDEN + 8, 256), F32),
        pltpu.VMEM((HIDDEN + 8, 256), F32),
        pltpu.VMEM((5, CHANNELS, COLS), F32),
        pltpu.VMEM((CHANNELS, COLS), F32),
        pltpu.VMEM((ROWS, CHANNELS, COLS), F32),
        pltpu.VMEM((2, 2, MARGIN, PADDED, COLS), BF16),
        pltpu.VMEM((2, 2, MARGIN, PADDED, COLS), BF16),
        pltpu.VMEM((2, 112, COLS), BF16),
        pltpu.VMEM((2, 6, 112, COLS), BF16),
        pltpu.VMEM((2, GROUPS, CHIPS, 16, COLS), BF16),
        pltpu.VMEM((GROUPS, CHIPS, 16, COLS), BF16),
        pltpu.VMEM((GROUPS, CHIPS, 16, COLS), BF16),
        pltpu.VMEM((GROUPS, CHIPS, 16, COLS), BF16),
        pltpu.VMEM((128, COLS), F32),
        pltpu.VMEM((128, COLS), F32),
        pltpu.VMEM((GROUPS, 16, COLS), F32),
        pltpu.VMEM((GROUPS, 16, COLS), F32),
        pltpu.VMEM((CHIPS, 2, 16, COLS), BF16),
        pltpu.VMEM((CHIPS, 2, 16, COLS), BF16),
        pltpu.VMEM((GROUPS, 2, 16, COLS), F32),
        dma((2, 8)),
        dma((2, 8)),
        dma((2,)),
        dma((2,)),
        dma((GROUPS,)),
        dma((GROUPS,)),
        dma((GROUPS,)),
        dma((GROUPS,)),
        dma((CHIPS,)),
        dma((CHIPS,)),
        dma((GROUPS,)),
        dma((GROUPS,)),
    ]


def local(
    state_in,
    cotangent,
    ocean_mask,
    slot_column,
    dw_taps,
    dw_bias,
    norm_gain,
    norm_bias,
    up_weight,
    up_bias,
    down_weight,
    down_bias,
    layer_scale,
):
    vectors = jnp.stack([dw_bias, norm_gain, norm_bias, down_bias, layer_scale], axis=1)
    cols = jnp.concatenate([dw_taps, vectors], axis=1).astype(F32)
    up_wide = jnp.concatenate(
        [up_weight, up_bias[:, None], jnp.zeros((HIDDEN, PADDED - CHANNELS - 1), BF16)], axis=1
    )
    vmem = pl.BlockSpec(memory_space=pltpu.VMEM)
    grad_rows, tail = pl.pallas_call(
        kernel,
        out_shape=(
            jax.ShapeDtypeStruct((ROWS, CHANNELS, COLS), BF16),
            jax.ShapeDtypeStruct((GROUPS, 2, 16, COLS), F32),
        ),
        in_specs=[pl.BlockSpec(memory_space=pltpu.SMEM)] + [vmem] * 6,
        out_specs=(vmem, vmem),
        scratch_shapes=scratch(),
        compiler_params=pltpu.CompilerParams(
            collective_id=0, has_side_effects=True, vmem_limit_bytes=60 * 1024 * 1024
        ),
    )(slot_column, ocean_mask[0], state_in[0], cotangent[0], cols, up_wide, down_weight)
    grad_state = grad_rows.transpose(1, 0, 2)[None]
    weights = tail[:, 0].reshape(2, 4, 16, COLS).transpose(0, 2, 1, 3).reshape(32, 4 * COLS)
    grad_up = weights[:SHARE, :CHANNELS]
    grad_up_bias = weights[:SHARE, CHANNELS]
    grad_down = weights[:SHARE, 2 * COLS : 2 * COLS + CHANNELS].T
    small = tail[:, 1].reshape(128, COLS)
    wide = jnp.concatenate([small[:FOLD, :64], small[: CHANNELS - FOLD, 64:]], axis=0)
    return (
        grad_state,
        grad_up,
        grad_up_bias,
        grad_down,
        wide[:, :TAPS],
        wide[:, TAPS : TAPS + 5].T,
    )


def solution(mesh):
    slots = P(("group", "tile"), None, None, None)
    in_specs = (slots, slots, P(("group", "tile"), None, None), P(("group", "tile"))) + (P(),) * 9
    out_specs = (slots, P("tile", None), P("tile"), P(None, "tile"), P(), P())
    return jax.shard_map(local, mesh=mesh, in_specs=in_specs, out_specs=out_specs, check_vma=False)
```

time: 362 us -> 76 us (0.21)
  the two profiles are of different devices: /device:TPU:1 before, /device:TPU:8 now
where the time goes in v1:
time: 76 us; the launch traced here: 75.7 us
  Pallas kernels  63.2 us (83%)
  local copies, waits for them, and re-layouts  8.2 us (11%)
  other arithmetic  2.96 us (4%)
  between operations  1.41 us (2%)
    pallas_call x1, Pallas kernels, local(): pl.pallas_call(kernel, out_shape=(jax.ShapeDtypeStruct((ROWS, CHANNELS, C...  63.2 us
    unnamed x22, local copies, waits for them, and re-layouts  5.02 us

profile of v1, /device:TPU:8, one launch (start us, length us, event | category | flops | bytes accessed | tf_op | source)
XLA Modules:
  0.0 75.7 jit_solution(8110634361886865508)
XLA Ops:
  0.6 0.0 copy-start.2
  0.6 1.2 %copy.31 = bf16[800,200]{1,0:T(8,128)(2,1)S(1)} copy(bf16[800,200]{0,1:T(8,128)(2,1)} %param.21) | data formatting | bytes 640000 | tf_op args[8]
  1.8 0.0 copy-done.2
  1.8 0.2 broadcast_in_dim.12
  2.0 0.1 pad.4.clone
  2.1 0.9 %maximum_maximum_fusion.upw_ref = bf16[800,208]{1,0:T(8,128)(2,1)} fusion(bf16[800,1]{1,0:T(8,128)(2,1)S(1)} %broadcast_in_dim.12, bf16[800,200]{1,0:T(8,128)(2,1)S(1)} %copy.31, bf16[208]{0:T(256)(128)(2,1)S(1)} %pad.4.clone), kind=kLoop, calls=%fused_computation | loop fusion | flops 998400 | bytes 654816 | tf_op jit(solution)/shard_map/concatenate | solution.py:634
  3.0 0.0 copy-done.1
  3.0 0.1 copy.25
  3.1 0.5 copy-done.3
  3.7 0.1 stack.20
  3.8 0.6 copy-done.4
  4.3 0.1 stack.21
  4.4 0.6 copy-done.5
  5.0 0.1 stack.22
  5.1 0.6 copy-done.6
  5.6 0.1 stack.23
  5.7 0.6 copy-done.7
  6.3 0.1 stack.24
  6.4 0.2 concatenate.9
  6.6 0.6 convert_element_type.3.cols_ref
  7.9 63.2 %shard_map.172 = (bf16[8,200,128]{2,1,0:T(8,128)(2,1)}, f32[8,2,16,128]{3,2,1,0:T(8,128)}) custom-call(s32[1]{0:T(128)S(6)} %copy.42.slot_ref, s32[8,128]{1,0:T(8,128)} %bitcast.28, bf16[200,8,128]{2,1,0:T(8,128)(2,1)} %bitcast.21, bf16[200,8,128]{2,1,0:T(8,128)(2,1)} %bitcast.22, f32[200,54]{1,0:T(8,128)} %convert_element_type.3.cols_ref, ...), custom_call_target="tpu_custom_call" | custom-call | tf_op jit(solution)/shard_map/pallas_call | solution.py:638
  71.0 0.9 %fusion.2 = (f32[8,1,16,128]{3,2,1,0:T(8,128)S(1)}, f32[8,1,16,128]{3,2,1,0:T(8,128)S(1)}) fusion(f32[8,2,16,128]{3,2,1,0:T(8,128)} %get-tuple-element.9), kind=kLoop, calls=%fused_computation.9 | loop fusion | bytes 262144 | tf_op jit(solution)/shard_map/slice | solution.py:656
  71.9 0.1 copy.37
  72.0 0.0 copy-start
  72.0 0.1 slice.40
  72.1 0.1 copy.38
  72.2 0.7 fusion.1
  72.9 0.7 fusion
  73.6 0.6 slice_bitcast_fusion
  74.2 0.7 slice_reduce_fusion
  74.9 0.0 copy-done
  74.9 0.8 %copy.36 = bf16[1,200,8,128]{3,2,1,0:T(8,128)(2,1)} copy(bf16[1,200,8,128]{3,1,2,0:T(8,128)(2,1)S(1)} %bitcast.23) | data formatting | bytes 819200
  (10 shorter events, 0.1 us)
Async XLA Ops:
  0.6 1.2 %copy-start.2 = (bf16[800]{0:T(1024)(128)(2,1)S(1)}, bf16[800]{0:T(1024)(128)(2,1)}, u32[]{:S(2)}) copy-start(bf16[800]{0:T(1024)(128)(2,1)} %param.22) | copy-start | bytes 4804
  2.1 0.9 %copy-start.1 = (bf16[200,49]{0,1:T(8,128)(2,1)S(1)}, bf16[200,49]{0,1:T(8,128)(2,1)}, u32[]{:S(2)}) copy-start(bf16[200,49]{0,1:T(8,128)(2,1)} %param.17) | copy-start | bytes 58804
  3.0 0.7 copy-start.3
  3.7 0.7 copy-start.4
  4.3 0.7 copy-start.5
  5.0 0.7 copy-start.6
  5.6 0.7 copy-start.7
  72.0 2.9 %copy-start = (bf16[8,200,128]{2,1,0:T(8,128)(2,1)S(1)}, bf16[8,200,128]{2,1,0:T(8,128)(2,1)}, u32[]{:S(2)}) copy-start(bf16[8,200,128]{2,1,0:T(8,128)(2,1)} %get-tuple-element.8) | copy-start | bytes 1228804

commit v2 on v1

v2 whole, which is shorter than its diff:
```python
import math

import jax
import jax.numpy as jnp
from jax import lax
from jax.experimental import pallas as pl
from jax.experimental.pallas import tpu as pltpu
from jax.sharding import PartitionSpec as P

MESH = pl.DeviceIdType.MESH
F32 = jnp.float32
BF16 = jnp.bfloat16

CHANNELS = 200
PADDED = 208
HIDDEN = 800
KERNEL = 7
TAPS = KERNEL * KERNEL
MARGIN = 3
ROWS = 8
COLS = 128
CELLS = ROWS * COLS
TALL = ROWS + 2 * MARGIN
BLOCKS = CHANNELS // 8
FOLD = 104
GROUPS = 8
TILES = 32
CHIPS = TILES // 2
PLACES = 2 * GROUPS
SHARE = HIDDEN // TILES
CHUNK = 80
UNROLL = 5
VMEM_BYTES = 60 * 1024 * 1024

NORM_EPSILON = 1e-06
SQRT_HALF = 0.7071067811865476
GAUSS_SCALE = 0.3989422804014327

DW_BIAS, GAIN, SHIFT, DOWN_BIAS, SCALE = range(TAPS, TAPS + 5)


def shift_lanes(column):
    place = column if column < MARGIN else column - 1
    return slice(place * COLS, (place + 1) * COLS)


def moved_row(field, kept, row, rows, column):
    if column == MARGIN:
        return field[row, rows, :]
    return kept[row, rows, shift_lanes(column)]


INNER = tuple(range(MARGIN, MARGIN + ROWS))
OUTER = tuple(range(MARGIN)) + tuple(range(MARGIN + ROWS, TALL))


def convolve(field, kept, taps, rows, flipped, sources, total):
    for column in range(KERNEL):
        moved = {row: moved_row(field, kept, row, rows, column) for row in sources}
        for tap_row in range(KERNEL):
            reached = [row for row in range(ROWS) if row + tap_row in moved]
            if not reached:
                continue
            index = tap_row * KERNEL + column
            weight = taps[TAPS - 1 - index if flipped else index, rows, :]
            for row in reached:
                term = weight * moved[row + tap_row]
                total[row] = term if total[row] is None else total[row] + term
    return total


def block_rows(block):
    return pl.ds(pl.multiple_of(block * 8, 8), 8)


def lane_slice(row):
    return pl.ds(pl.multiple_of(row * COLS, COLS), COLS)


def iota(shape, dim):
    return lax.broadcasted_iota(jnp.int32, shape, dim)


def kernel(
    slot_ref,
    mask_ref,
    state_ref,
    cot_ref,
    taps_ref,
    upw_ref,
    downw_ref,
    bias_ref,
    gain_ref,
    shift_ref,
    dbias_ref,
    scale_ref,
    ubias_ref,
    gs_ref,
    tail_ref,
    mask_v,
    state_v,
    cot_v,
    taps_v,
    upw_v,
    downw_v,
    bias_v,
    gain_v,
    shift_v,
    dbias_v,
    scale_v,
    ubias_v,
    cols,
    moves,
    turns,
    flat,
    ext,
    exg,
    wide,
    taps,
    kept,
    normed,
    spread,
    mgrad,
    nlow,
    gblow,
    act,
    gpre,
    branch,
    gnorm,
    up_t,
    up_w,
    down_t,
    gup,
    gdown,
    sums,
    small_wide,
    gstate,
    rows_send,
    rows_recv,
    pack_send,
    pack_recv,
    w_send,
    w_core,
    w_group,
    w_group_in,
    w_tile,
    w_tile_in,
    w_final,
    small,
    small_in,
    s_tile,
    s_tile_in,
    s_final,
    load_sem,
    store_sem,
    halo_ssem,
    halo_rsem,
    core_ssem,
    core_rsem,
    wgroup_ssem,
    wgroup_rsem,
    small_ssem,
    small_rsem,
    wtile_ssem,
    wtile_rsem,
    stile_ssem,
    stile_rsem,
    wfinal_ssem,
    wfinal_rsem,
    sfinal_ssem,
    sfinal_rsem,
):
    g = lax.axis_index("group")
    t = lax.axis_index("tile")
    core = lax.rem(t, 2)
    chip = t // 2
    partner = chip * 2 + 1 - core
    place = g * 2 + core
    east = lax.rem(t + 1, TILES)
    west = lax.rem(t + TILES - 1, TILES)
    has_above = g > 0
    has_below = g < GROUPS - 1

    def remote(source, target, send, recv, gg, tt):
        return pltpu.make_async_remote_copy(
            src_ref=source,
            dst_ref=target,
            send_sem=send,
            recv_sem=recv,
            device_id=(gg, tt),
            device_id_type=MESH,
        )

    def finished(copy):
        copy.wait_send()
        copy.wait_recv()

    barrier = pltpu.get_barrier_semaphore()

    def greet(gg, tt):
        pl.semaphore_signal(barrier, inc=1, device_id=(gg, tt), device_id_type=MESH)

    def other_place(k):
        other = lax.rem(place + k, PLACES)
        return other // 2, chip * 2 + lax.rem(other, 2), other

    greet(g, east)
    greet(g, west)

    @pl.when(has_above)
    def _():
        greet(g - 1, east)
        greet(g - 1, west)

    @pl.when(has_below)
    def _():
        greet(g + 1, east)
        greet(g + 1, west)

    for k in range(1, PLACES):
        greet(*other_place(k)[:2])
    for k in range(1, CHIPS):
        greet(g, lax.rem(chip + k, CHIPS) * 2 + core)

    loads = [
        pltpu.make_async_copy(source, target, load_sem.at[index])
        for index, (source, target) in enumerate(
            [
                (state_ref, state_v),
                (mask_ref, mask_v),
                (taps_ref, taps_v),
                (bias_ref, bias_v),
                (gain_ref, gain_v),
                (shift_ref, shift_v),
                (dbias_ref, dbias_v),
                (scale_ref, scale_v),
                (cot_ref, cot_v),
                (upw_ref, upw_v),
                (ubias_ref, ubias_v),
                (downw_ref, downw_v),
            ]
        )
    ]
    for copy in loads:
        copy.start()

    def halo_copies(phase):
        def rows_copy(slot, gg):
            return remote(
                rows_send.at[phase, slot],
                rows_recv.at[phase, slot],
                halo_ssem.at[phase, slot],
                halo_rsem.at[phase, slot],
                gg,
                t,
            )

        def pack_copy(slot, gg, tt):
            return remote(
                pack_send.at[phase],
                pack_recv.at[phase, slot],
                halo_ssem.at[phase, 2 + slot],
                halo_rsem.at[phase, 2 + slot],
                gg,
                tt,
            )

        side = [pack_copy(0, g, west), pack_copy(1, g, east)]
        down = [rows_copy(0, g + 1), pack_copy(2, g + 1, west), pack_copy(3, g + 1, east)]
        up = [rows_copy(1, g - 1), pack_copy(4, g - 1, west), pack_copy(5, g - 1, east)]
        return side, down, up

    def halo_start(phase):
        side, down, up = halo_copies(phase)
        for copy in side:
            copy.start()

        @pl.when(has_below)
        def _():
            for copy in down:
                copy.start()

        @pl.when(has_above)
        def _():
            for copy in up:
                copy.start()

    def halo_wait_sides(phase):
        for copy in halo_copies(phase)[0]:
            finished(copy)

    def halo_wait_rest(phase):
        _, down, up = halo_copies(phase)

        @pl.when(has_below)
        def _():
            for copy in down:
                copy.wait_send()
            for copy in up:
                copy.wait_recv()

        @pl.when(has_above)
        def _():
            for copy in up:
                copy.wait_send()
            for copy in down:
                copy.wait_recv()

    def pack_up(phase, field):
        lane = iota((CHANNELS, COLS), 1)
        spot = lax.rem(lane + 3, COLS) // 8
        pack = field[MARGIN]
        for row in range(1, ROWS):
            pack = jnp.where(spot == row, pltpu.roll(field[MARGIN + row], 8 * row, 1), pack)
        second = pltpu.roll(pack[FOLD:], 64, 1)
        lane = iota((CHANNELS - FOLD, COLS), 1)
        first = jnp.where((lane >= 61) & (lane < 125), second, pack[: CHANNELS - FOLD])
        zeros = jnp.zeros((8, COLS), F32)
        whole = jnp.concatenate([first, pack[CHANNELS - FOLD : FOLD], zeros], axis=0)
        pack_send[phase] = whole.astype(BF16)
        pad = jnp.zeros((MARGIN, PADDED - CHANNELS, COLS), BF16)
        bottom = field[ROWS : ROWS + MARGIN].astype(BF16)
        top = field[MARGIN : 2 * MARGIN].astype(BF16)
        rows_send[phase, 0] = jnp.concatenate([bottom, pad], axis=1)
        rows_send[phase, 1] = jnp.concatenate([top, pad], axis=1)

    def unfold(phase, index):
        lane = iota((112, COLS), 1)
        from_east = pack_recv[phase, 2 * index].astype(F32)
        from_west = pack_recv[phase, 2 * index + 1].astype(F32)
        both = jnp.where(lax.rem(lane, 8) < 4, from_east, from_west)[:FOLD]
        return jnp.concatenate([both, pltpu.roll(both, 64, 1)], axis=0).astype(BF16)

    def move_inner(phase, field):
        for row in INNER:
            wide[row, :CHANNELS, :COLS] = field[row].astype(BF16)
        sides = jnp.dot(unfold(phase, 0), turns[...], preferred_element_type=F32).astype(BF16)
        for row in range(ROWS):
            wide[MARGIN + row, :, COLS:] = sides[:, row * COLS : (row + 1) * COLS]
        cells = wide[MARGIN : MARGIN + ROWS].reshape(ROWS * PADDED, 2 * COLS)
        out = jnp.dot(cells, moves[...], preferred_element_type=F32)
        kept[MARGIN : MARGIN + ROWS] = out.reshape(ROWS, PADDED, (KERNEL - 1) * COLS)

    def move_outer(phase, field):
        for index, first, begin in ((0, 0, ROWS - MARGIN), (1, MARGIN + ROWS, 0)):
            rows = rows_recv[phase, index]
            wide[first : first + MARGIN, :, :COLS] = rows
            field[first : first + MARGIN] = rows[:, :CHANNELS].astype(F32)
            turn = turns[:, begin * COLS : (begin + MARGIN) * COLS]
            sides = jnp.dot(unfold(phase, 1 + index), turn, preferred_element_type=F32)
            sides = sides.astype(BF16)
            for row in range(MARGIN):
                wide[first + row, :, COLS:] = sides[:, row * COLS : (row + 1) * COLS]
            cells = wide[first : first + MARGIN].reshape(MARGIN * PADDED, 2 * COLS)
            out = jnp.dot(cells, moves[...], preferred_element_type=F32)
            kept[first : first + MARGIN] = out.reshape(MARGIN, PADDED, (KERNEL - 1) * COLS)

    @pl.when(jnp.logical_not(has_above))
    def _():
        for phase in range(2):
            rows_recv[phase, 0] = jnp.zeros((MARGIN, PADDED, COLS), BF16)
            pack_recv[phase, 2] = jnp.zeros((112, COLS), BF16)
            pack_recv[phase, 3] = jnp.zeros((112, COLS), BF16)

    @pl.when(jnp.logical_not(has_below))
    def _():
        for phase in range(2):
            rows_recv[phase, 1] = jnp.zeros((MARGIN, PADDED, COLS), BF16)
            pack_recv[phase, 4] = jnp.zeros((112, COLS), BF16)
            pack_recv[phase, 5] = jnp.zeros((112, COLS), BF16)

    source = iota((2 * COLS, COLS), 0)
    lane = iota((2 * COLS, COLS), 1)
    for column in range(KERNEL):
        if column == MARGIN:
            continue
        wanted = lane + (column - MARGIN)
        beside = (wanted < 0) | (wanted >= COLS)
        wanted = jnp.where(beside, COLS + lax.rem(wanted + COLS, COLS), wanted)
        moves[:, shift_lanes(column)] = (source == wanted).astype(F32).astype(BF16)
    source = iota((COLS, COLS), 0)
    lane = iota((COLS, COLS), 1)
    edge = (lane < MARGIN) | (lane >= COLS - MARGIN)
    for row in range(ROWS):
        hit = edge & (source == lax.rem(lane + 8 * row, COLS))
        turns[:, row * COLS : (row + 1) * COLS] = hit.astype(F32).astype(BF16)

    live = (slot_ref[0] >= 0).astype(F32)
    loads[1].wait()
    loads[0].wait()
    mask = mask_v[...].astype(F32) * live
    flat[...] = (state_v[...].astype(F32) * mask[None]).reshape(CHANNELS * ROWS, COLS)
    for row in range(ROWS):
        ext[MARGIN + row] = flat[pl.ds(row, CHANNELS, stride=ROWS), :]
    pack_up(0, ext)

    for copy in loads[2:8]:
        copy.wait()
    vectors = [ref[...].astype(F32).reshape(1, CHANNELS) for ref in (bias_v, gain_v, shift_v, dbias_v, scale_v)]
    lines = [taps_v[...].astype(F32)] + vectors + [jnp.zeros((2, CHANNELS), F32)]
    cols[...] = jnp.concatenate(lines, axis=0).T
    for tap in range(TAPS):
        taps[tap] = jnp.broadcast_to(cols[:, tap : tap + 1], (CHANNELS, COLS))

    met = 2 + (PLACES - 1) + (CHIPS - 1)
    met = met + 2 * has_above.astype(jnp.int32) + 2 * has_below.astype(jnp.int32)
    pl.semaphore_wait(barrier, met)

    halo_start(0)
    loads[8].wait()
    flat[...] = (cot_v[...].astype(F32) * mask[None]).reshape(CHANNELS * ROWS, COLS)
    scale_col = cols[:, SCALE : SCALE + 1]
    for row in range(ROWS):
        masked = flat[pl.ds(row, CHANNELS, stride=ROWS), :]
        mgrad[row] = masked
        gblow[:, row * COLS : (row + 1) * COLS] = (masked * scale_col).astype(BF16)
    for copy in loads[9:]:
        copy.wait()
    bias_line = ubias_v[...].reshape(1, HIDDEN)
    below = jnp.where(iota((PADDED - CHANNELS, HIDDEN), 0) == 0, bias_line.astype(F32), 0.0)
    up_t[...] = jnp.concatenate([upw_v[...], below.astype(BF16)], axis=0)
    up_w[...] = up_t[...].T
    down_t[...] = downw_v[...].T

    halo_wait_sides(0)

    move_inner(0, ext)

    @pl.loop(0, BLOCKS, unroll=UNROLL)
    def _(block):
        rows = block_rows(block)
        total = convolve(ext, kept, taps, rows, False, INNER, [None] * ROWS)
        for row in range(ROWS):
            normed[row, rows, :] = total[row]

    halo_wait_rest(0)

    move_outer(0, ext)

    @pl.loop(0, BLOCKS, unroll=UNROLL)
    def _(block):
        rows = block_rows(block)
        total = [normed[row, rows, :] for row in range(ROWS)]
        total = convolve(ext, kept, taps, rows, False, OUTER, total)
        bias = cols[rows, DW_BIAS : DW_BIAS + 1]
        for row in range(ROWS):
            normed[row, rows, :] = (total[row] * live + bias).astype(BF16).astype(F32)

    gain_col = cols[:, GAIN : GAIN + 1]
    shift_col = cols[:, SHIFT : SHIFT + 1]

    @pl.loop(0, ROWS)
    def _(row):
        conv = normed[row]
        offset = conv - jnp.mean(conv, axis=0, keepdims=True)
        rate = lax.rsqrt(jnp.mean(offset * offset, axis=0, keepdims=True) + NORM_EPSILON)
        unit = offset * rate
        spread[row] = rate
        normed[row] = unit
        low = (unit * gain_col + shift_col).astype(BF16)
        tail = (iota((PADDED - CHANNELS, COLS), 0) == 0).astype(F32).astype(BF16)
        nlow[:, lane_slice(row)] = jnp.concatenate([low, tail], axis=0)

    @pl.loop(0, HIDDEN // CHUNK)
    def _(chunk):
        units = pl.ds(pl.multiple_of(chunk * CHUNK, CHUNK), CHUNK)
        pre = jnp.dot(up_w[units, :], nlow[...], preferred_element_type=F32)
        mass = 0.5 * (1.0 + lax.erf(pre * SQRT_HALF))
        density = GAUSS_SCALE * jnp.exp(-0.5 * pre * pre)
        act[units, :] = (pre * mass).astype(BF16)
        grad_act = jnp.dot(down_t[units, :], gblow[...], preferred_element_type=F32)
        gpre[units, :] = (grad_act * (mass + pre * density)).astype(BF16)

    branch[...] = jnp.dot(downw_v[...], act[...], preferred_element_type=F32)
    gnorm[...] = jnp.dot(up_t[...], gpre[...], preferred_element_type=F32)[:CHANNELS]

    sums[...] = jnp.zeros_like(sums)
    down_bias = cols[:, DOWN_BIAS : DOWN_BIAS + 1]

    @pl.loop(0, ROWS)
    def _(row):
        grad = gnorm[:, lane_slice(row)]
        unit = normed[row]
        masked = mgrad[row]
        sums[1] += grad * unit
        sums[2] += grad
        sums[3] += masked * scale_col
        sums[4] += masked * (branch[:, lane_slice(row)] + down_bias)
        scaled = grad * gain_col
        first = jnp.mean(scaled, axis=0, keepdims=True)
        second = jnp.mean(scaled * unit, axis=0, keepdims=True)
        low = (spread[row] * (scaled - first - unit * second)).astype(BF16).astype(F32)
        exg[MARGIN + row] = low
        sums[0] += low

    pack_up(1, exg)
    halo_start(1)

    trans = (((1,), (1,)), ((), ()))
    gup[:HIDDEN, :PADDED] = lax.dot_general(gpre[...], nlow[...], trans, preferred_element_type=F32)
    gdown[:HIDDEN, :CHANNELS] = lax.dot_general(
        act[...], gblow[...], trans, preferred_element_type=F32
    )

    for tile in range(TILES):
        for half in range(2):
            begin = tile * SHARE + 16 * half
            for part in range(4):
                source = gup if part < 2 else gdown
                side = (part % 2) * COLS
                piece = source[begin : begin + 16, side : side + COLS]
                if begin + 16 > HIDDEN:
                    piece = jnp.where(iota((16, COLS), 0) < HIDDEN - begin, piece, 0.0)
                w_send[tile % 2, half * 4 + part, tile // 2] = piece.astype(BF16)

    w_core_copy = remote(
        w_send.at[1 - core], w_core, core_ssem.at[0], core_rsem.at[0], g, partner
    )
    w_core_copy.start()

    def tap_block(block):
        rows = block_rows(block)
        lane = iota((8, COLS), 1)
        own = [exg[MARGIN + row, rows, :] for row in range(ROWS)]
        out = jnp.zeros((8, COLS), F32)
        for column in range(KERNEL):
            moved = [moved_row(ext, kept, row, rows, column) for row in range(TALL)]
            for tap_row in range(KERNEL):
                total = own[0] * moved[tap_row]
                for row in range(1, ROWS):
                    total = total + own[row] * moved[row + tap_row]
                spot = lane == tap_row * KERNEL + column
                out = jnp.where(spot, jnp.sum(total, axis=1, keepdims=True), out)
        for vector in range(5):
            total = jnp.sum(sums[vector, rows, :], axis=1, keepdims=True)
            out = jnp.where(lane == TAPS + vector, total, out)
        small_wide[rows, :] = out * live

    pl.loop(0, 10, unroll=UNROLL)(tap_block)

    finished(w_core_copy)

    @pl.loop(0, GROUPS)
    def _(piece):
        total = w_send[core, piece].astype(F32) + w_core[piece].astype(F32)
        w_group[piece] = total.astype(BF16)

    def w_group_copy(k):
        other = lax.rem(g + k, GROUPS)
        return remote(
            w_group.at[other], w_group_in.at[k], wgroup_ssem.at[k], wgroup_rsem.at[k], other, t
        )

    for k in range(1, GROUPS):
        w_group_copy(k).start()

    pl.loop(10, BLOCKS, unroll=UNROLL)(tap_block)

    second = pltpu.roll(small_wide[FOLD:], 64, 1)
    whole = jnp.concatenate(
        [
            small_wide[: CHANNELS - FOLD] + second,
            small_wide[CHANNELS - FOLD : FOLD],
            jnp.zeros((128 - FOLD, COLS), F32),
        ],
        axis=0,
    )
    small[...] = whole.reshape(PLACES, 8, COLS)

    def s_copy(k):
        gg, tt, other = other_place(k)
        return remote(small.at[other], small_in.at[k], small_ssem.at[k], small_rsem.at[k], gg, tt)

    for k in range(1, PLACES):
        s_copy(k).start()

    halo_wait_sides(1)

    move_inner(1, exg)

    def finish_inner(block):
        rows = block_rows(block)
        total = convolve(exg, kept, taps, rows, True, INNER, [None] * ROWS)
        for row in range(ROWS):
            gstate[row, rows, :] = total[row]

    def finish_outer(block):
        rows = block_rows(block)
        total = [gstate[row, rows, :] for row in range(ROWS)]
        total = convolve(exg, kept, taps, rows, True, OUTER, total)
        for row in range(ROWS):
            cell = mask[row : row + 1]
            spots = pl.ds(block * 64 + row, 8, stride=ROWS)
            flat[spots, :] = cell * (mgrad[row, rows, :] + total[row])

    pl.loop(0, 10, unroll=UNROLL)(finish_inner)

    total = w_group[g].astype(F32)
    for k in range(1, GROUPS):
        finished(w_group_copy(k))
        total = total + w_group_in[k].astype(F32)
    w_tile[...] = total.astype(BF16)

    def w_tile_copy(k):
        other = lax.rem(chip + k, CHIPS)
        return remote(
            w_tile.at[other],
            w_tile_in.at[chip],
            wtile_ssem.at[k],
            wtile_rsem.at[k],
            g,
            other * 2 + core,
        )

    for k in range(1, CHIPS):
        w_tile_copy(k).start()

    total = small[place]
    for k in range(1, PLACES):
        finished(s_copy(k))
        total = total + small_in[k]
    s_tile[...] = total

    def s_tile_copy(k):
        other = lax.rem(chip + k, CHIPS)
        return remote(
            s_tile, s_tile_in.at[chip], stile_ssem.at[k], stile_rsem.at[k], g, other * 2 + core
        )

    for k in range(1, CHIPS):
        s_tile_copy(k).start()

    pl.loop(10, BLOCKS, unroll=UNROLL)(finish_inner)

    halo_wait_rest(1)

    move_outer(1, exg)

    w_tile_in[chip] = w_tile[chip]
    for k in range(1, CHIPS):
        finished(w_tile_copy(k))
    total = w_tile_in[0].astype(F32)
    for other in range(1, CHIPS):
        total = total + w_tile_in[other].astype(F32)
    w_final[g] = total

    def w_final_copy(k):
        other = lax.rem(g + k, GROUPS)
        return remote(w_final.at[g], w_final.at[g], wfinal_ssem.at[k], wfinal_rsem.at[k], other, t)

    for k in range(1, GROUPS):
        w_final_copy(k).start()

    s_tile_in[chip] = s_tile[...]
    for k in range(1, CHIPS):
        finished(s_tile_copy(k))
    total = s_tile_in[0]
    for other in range(1, CHIPS):
        total = total + s_tile_in[other]
    s_final[place] = total

    def s_final_copy(k):
        gg, tt, _ = other_place(k)
        return remote(
            s_final.at[place], s_final.at[place], sfinal_ssem.at[k], sfinal_rsem.at[k], gg, tt
        )

    for k in range(1, PLACES):
        s_final_copy(k).start()

    pl.loop(0, BLOCKS, unroll=UNROLL)(finish_outer)

    state_v[...] = flat[...].reshape(CHANNELS, ROWS, COLS).astype(BF16)
    store = pltpu.make_async_copy(state_v, gs_ref, store_sem)
    store.start()

    for k in range(1, GROUPS):
        finished(w_final_copy(k))
    for k in range(1, PLACES):
        finished(s_final_copy(k))
    factor = 1.0 / math.sqrt(CELLS * GROUPS * TILES)
    tail_ref[0] = w_final[...].reshape(128, COLS) * factor
    tail_ref[1] = s_final[...].reshape(128, COLS) * factor
    store.wait()


def scratch():
    dma = pltpu.SemaphoreType.DMA
    tile = (CHANNELS, ROWS, COLS)
    rows = (ROWS, CHANNELS, COLS)
    tall = (TALL, CHANNELS, COLS)
    pieces = (GROUPS, CHIPS, 16, COLS)
    return [
        pltpu.VMEM((ROWS, COLS), jnp.int32),
        pltpu.VMEM(tile, BF16),
        pltpu.VMEM(tile, BF16),
        pltpu.VMEM((TAPS, CHANNELS), BF16),
        pltpu.VMEM((CHANNELS, HIDDEN), BF16),
        pltpu.VMEM((CHANNELS, HIDDEN), BF16),
        pltpu.VMEM((CHANNELS,), BF16),
        pltpu.VMEM((CHANNELS,), BF16),
        pltpu.VMEM((CHANNELS,), BF16),
        pltpu.VMEM((CHANNELS,), BF16),
        pltpu.VMEM((CHANNELS,), BF16),
        pltpu.VMEM((HIDDEN,), BF16),
        pltpu.VMEM((CHANNELS, 56), F32),
        pltpu.VMEM((2 * COLS, (KERNEL - 1) * COLS), BF16),
        pltpu.VMEM((COLS, ROWS * COLS), BF16),
        pltpu.VMEM((CHANNELS * ROWS, COLS), F32),
        pltpu.VMEM(tall, F32),
        pltpu.VMEM(tall, F32),
        pltpu.VMEM((TALL, PADDED, 2 * COLS), BF16),
        pltpu.VMEM((TAPS, CHANNELS, COLS), F32),
        pltpu.VMEM((TALL, PADDED, (KERNEL - 1) * COLS), F32),
        pltpu.VMEM(rows, F32),
        pltpu.VMEM((ROWS, 1, COLS), F32),
        pltpu.VMEM(rows, F32),
        pltpu.VMEM((PADDED, CELLS), BF16),
        pltpu.VMEM((CHANNELS, CELLS), BF16),
        pltpu.VMEM((HIDDEN, CELLS), BF16),
        pltpu.VMEM((HIDDEN, CELLS), BF16),
        pltpu.VMEM((CHANNELS, CELLS), F32),
        pltpu.VMEM((CHANNELS, CELLS), F32),
        pltpu.VMEM((PADDED, HIDDEN), BF16),
        pltpu.VMEM((HIDDEN, PADDED), BF16),
        pltpu.VMEM((HIDDEN, CHANNELS), BF16),
        pltpu.VMEM((HIDDEN + 8, 256), F32),
        pltpu.VMEM((HIDDEN + 8, 256), F32),
        pltpu.VMEM((5, CHANNELS, COLS), F32),
        pltpu.VMEM((CHANNELS, COLS), F32),
        pltpu.VMEM(rows, F32),
        pltpu.VMEM((2, 2, MARGIN, PADDED, COLS), BF16),
        pltpu.VMEM((2, 2, MARGIN, PADDED, COLS), BF16),
        pltpu.VMEM((2, 112, COLS), BF16),
        pltpu.VMEM((2, 6, 112, COLS), BF16),
        pltpu.VMEM((2,) + pieces, BF16),
        pltpu.VMEM(pieces, BF16),
        pltpu.VMEM(pieces, BF16),
        pltpu.VMEM(pieces, BF16),
        pltpu.VMEM((CHIPS, 16, COLS), BF16),
        pltpu.VMEM((CHIPS, 16, COLS), BF16),
        pltpu.VMEM((GROUPS, 16, COLS), F32),
        pltpu.VMEM((PLACES, 8, COLS), F32),
        pltpu.VMEM((PLACES, 8, COLS), F32),
        pltpu.VMEM((8, COLS), F32),
        pltpu.VMEM((CHIPS, 8, COLS), F32),
        pltpu.VMEM((PLACES, 8, COLS), F32),
        dma((12,)),
        dma(()),
        dma((2, 8)),
        dma((2, 8)),
        dma((1,)),
        dma((1,)),
        dma((GROUPS,)),
        dma((GROUPS,)),
        dma((PLACES,)),
        dma((PLACES,)),
        dma((CHIPS,)),
        dma((CHIPS,)),
        dma((CHIPS,)),
        dma((CHIPS,)),
        dma((GROUPS,)),
        dma((GROUPS,)),
        dma((PLACES,)),
        dma((PLACES,)),
    ]


def place_results(
    rows_ref, tail_ref, gs_ref, up_ref, ubias_ref, down_ref, taps_ref, vec_ref, rows, sems
):
    load = pltpu.make_async_copy(rows_ref, rows, sems.at[0])
    load.start()
    for half, size in ((0, 16), (1, SHARE - 16)):
        for part in range(4):
            piece = tail_ref[0, (half * 4 + part) * 16 : (half * 4 + part) * 16 + size, :]
            target = up_ref if part < 2 else down_ref
            begin = (part % 2) * COLS
            width = min(COLS, CHANNELS - begin)
            target[half * 16 : half * 16 + size, begin : begin + width] = piece[:, :width]
    load.wait()
    copy = pltpu.make_async_copy(rows, gs_ref, sems.at[1])
    copy.start()
    edge = jnp.concatenate([tail_ref[0, 16:32, :], tail_ref[0, 80:96, :]], axis=0)
    line = edge.T[CHANNELS - COLS : CHANNELS - COLS + 1, :SHARE]
    ubias_ref[...] = line.reshape(SHARE)
    turned = tail_ref[1].T
    low, high = turned[:64, :FOLD], turned[64:, : CHANNELS - FOLD]
    every = jnp.concatenate([low, high], axis=1)
    taps_ref[...] = every[:TAPS]
    vec_ref[...] = every[TAPS : TAPS + 5]
    copy.wait()


def local(
    state_in,
    cotangent,
    ocean_mask,
    slot_column,
    dw_taps,
    dw_bias,
    norm_gain,
    norm_bias,
    up_weight,
    up_bias,
    down_weight,
    down_bias,
    layer_scale,
):
    vmem = pl.BlockSpec(memory_space=pltpu.VMEM)
    anywhere = pl.BlockSpec(memory_space=pl.ANY)
    grad_rows, tail = pl.pallas_call(
        kernel,
        out_shape=(
            jax.ShapeDtypeStruct((CHANNELS, ROWS, COLS), BF16),
            jax.ShapeDtypeStruct((2, 128, COLS), F32),
        ),
        in_specs=[pl.BlockSpec(memory_space=pltpu.SMEM)] + [anywhere] * 12,
        out_specs=(anywhere, vmem),
        scratch_shapes=scratch(),
        compiler_params=pltpu.CompilerParams(
            collective_id=0, has_side_effects=True, vmem_limit_bytes=VMEM_BYTES
        ),
    )(
        slot_column,
        ocean_mask[0],
        state_in[0],
        cotangent[0],
        dw_taps.T,
        up_weight.T,
        down_weight,
        dw_bias,
        norm_gain,
        norm_bias,
        down_bias,
        layer_scale,
        up_bias,
    )
    grad_state, grad_up, grad_up_bias, grad_down, grad_taps, grad_vectors = pl.pallas_call(
        place_results,
        out_shape=(
            jax.ShapeDtypeStruct((CHANNELS, ROWS, COLS), BF16),
            jax.ShapeDtypeStruct((SHARE, CHANNELS), F32),
            jax.ShapeDtypeStruct((SHARE,), F32),
            jax.ShapeDtypeStruct((SHARE, CHANNELS), F32),
            jax.ShapeDtypeStruct((TAPS, CHANNELS), F32),
            jax.ShapeDtypeStruct((5, CHANNELS), F32),
        ),
        in_specs=[anywhere, vmem],
        out_specs=(anywhere,) + (vmem,) * 5,
        scratch_shapes=[pltpu.VMEM((CHANNELS, ROWS, COLS), BF16), pltpu.SemaphoreType.DMA((2,))],
    )(grad_rows, tail)
    return grad_state[None], grad_up, grad_up_bias, grad_down.T, grad_taps.T, grad_vectors


def solution(mesh):
    slots = P(("group", "tile"), None, None, None)
    in_specs = (slots, slots, P(("group", "tile"), None, None), P(("group", "tile"))) + (P(),) * 9
    out_specs = (slots, P("tile", None), P("tile"), P(None, "tile"), P(), P())
    return jax.shard_map(local, mesh=mesh, in_specs=in_specs, out_specs=out_specs, check_vma=False)
```

time: 76 us -> 61.4 us (0.81)
  the two profiles are of different devices: /device:TPU:8 before, /device:TPU:1 now
where the time goes in v2:
time: 61.4 us; the launch traced here: 61.2 us
  Pallas kernels  59.8 us (97%)
  between operations  1.45 us (2%)
    pallas_call x1, Pallas kernels, local(): pl.pallas_call(kernel, out_shape=(jax.ShapeDtypeStruct((CHANNELS, ROWS, C...  56.4 us
    pallas_call x1, Pallas kernels, local(): pl.pallas_call(place_results, out_shape=(jax.ShapeDtypeStruct((CHANNELS,...  3.32 us

profile of v2, /device:TPU:1, one launch (start us, length us, event | category | flops | bytes accessed | tf_op | source)
XLA Modules:
  0.0 61.2 jit_solution(10761056149558101986)
XLA Ops:
  1.3 56.4 %shard_map.172 = (bf16[200,8,128]{2,1,0:T(8,128)(2,1)}, f32[2,128,128]{2,1,0:T(8,128)}) custom-call(s32[1]{0:T(128)S(6)} %copy.19.slot_ref, s32[8,128]{1,0:T(8,128)} %bitcast.12, bf16[200,8,128]{2,1,0:T(8,128)(2,1)} %bitcast.8, bf16[200,8,128]{2,1,0:T(8,128)(2,1)} %bitcast.9, bf16[49,200]{1,0:T(8,128)(2,1)} %bitcast.11, bf16[200,800]{1,0:T(8,128)(2,1)} %bitcast.10, ...), custom_call_target="tpu_custom_call" | custom-call | tf_op jit(solution)/shard_map/pallas_call | solution.py:812
  57.7 3.3 %shard_map.173 = (bf16[200,8,128]{2,1,0:T(8,128)(2,1)}, f32[25,200]{1,0:T(8,128)}, f32[25]{0:T(128)}, f32[25,200]{1,0:T(8,128)}, f32[49,200]{1,0:T(8,128)}, /*index=5*/f32[5,200]{1,0:T(8,128)}) custom-call(bf16[200,8,128]{2,1,0:T(8,128)(2,1)} %get-tuple-element.14.rows_ref, f32[2,128,128]{2,1,0:T(8,128)} %get-tuple-element.15.tail_ref), custom_call_target="tpu_custom_call" | custom-call | tf_op jit(solution)/shard_map/pallas_call | solution.py:839

commit v3 on v2

--- a/solution.py
+++ b/solution.py
@@ -24,11 +24,14 @@
 BLOCKS = CHANNELS // 8
 FOLD = 104
 GROUPS = 8
+DEPTH = 8
+LINE = 4
 TILES = 32
 CHIPS = TILES // 2
+PLANE = 2 * CHIPS
 PLACES = 2 * GROUPS
 SHARE = HIDDEN // TILES
-CHUNK = 80
+CHUNK = 400
 UNROLL = 5
 VMEM_BYTES = 60 * 1024 * 1024
 
@@ -176,6 +179,14 @@
     chip = t // 2
     partner = chip * 2 + 1 - core
     place = g * 2 + core
+    line = lax.rem(g, LINE)
+    low = g // LINE
+    plane = low * CHIPS + chip
+    depth = chip // 2
+    high = lax.rem(chip, 2)
+    pillar = high * 2 + low
+    sheet = line * DEPTH + depth
+    upper = depth // 4
     east = lax.rem(t + 1, TILES)
     west = lax.rem(t + TILES - 1, TILES)
     has_above = g > 0
@@ -191,6 +202,10 @@
             device_id_type=MESH,
         )
 
+    def all_finished(buffer, count, send, recv):
+        slots = buffer.at[pl.ds(0, count)]
+        finished(remote(slots, slots, send, recv, g, partner))
+
     def finished(copy):
         copy.wait_send()
         copy.wait_recv()
@@ -207,20 +222,16 @@
     greet(g, east)
     greet(g, west)
 
-    @pl.when(has_above)
-    def _():
-        greet(g - 1, east)
-        greet(g - 1, west)
-
-    @pl.when(has_below)
-    def _():
-        greet(g + 1, east)
-        greet(g + 1, west)
-
     for k in range(1, PLACES):
         greet(*other_place(k)[:2])
     for k in range(1, CHIPS):
-        greet(g, lax.rem(chip + k, CHIPS) * 2 + core)
+        other = lax.rem(chip + k, CHIPS) * 2 + core
+        greet(g, other)
+        greet(lax.rem(g + LINE, GROUPS), other)
+    for k in range(1, LINE):
+        for j in range(1, DEPTH):
+            other = lax.rem(depth + j, DEPTH) * 2 + high
+            greet(low * LINE + lax.rem(line + k, LINE), other * 2 + core)
 
     loads = [
         pltpu.make_async_copy(source, target, load_sem.at[index])
@@ -255,9 +266,9 @@
                 t,
             )
 
-        def pack_copy(slot, gg, tt):
+        def pack_copy(source, slot, gg, tt):
             return remote(
-                pack_send.at[phase],
+                pack_send.at[phase, source],
                 pack_recv.at[phase, slot],
                 halo_ssem.at[phase, 2 + slot],
                 halo_rsem.at[phase, 2 + slot],
@@ -265,25 +276,25 @@
                 tt,
             )
 
-        side = [pack_copy(0, g, west), pack_copy(1, g, east)]
-        down = [rows_copy(0, g + 1), pack_copy(2, g + 1, west), pack_copy(3, g + 1, east)]
-        up = [rows_copy(1, g - 1), pack_copy(4, g - 1, west), pack_copy(5, g - 1, east)]
+        side = [pack_copy(0, 0, g, west), pack_copy(0, 1, g, east)]
+        down = [rows_copy(0, g + 1), pack_copy(1, 2, g + 1, t)]
+        up = [rows_copy(1, g - 1), pack_copy(1, 3, g - 1, t)]
         return side, down, up
 
-    def halo_start(phase):
-        side, down, up = halo_copies(phase)
-        for copy in side:
+    def halo_start_sides(phase):
+        for copy in halo_copies(phase)[0]:
             copy.start()
+
+    def halo_start_rest(phase, which):
+        _, down, up = halo_copies(phase)
 
         @pl.when(has_below)
         def _():
-            for copy in down:
-                copy.start()
+            down[which].start()
 
         @pl.when(has_above)
         def _():
-            for copy in up:
-                copy.start()
+            up[which].start()
 
     def halo_wait_sides(phase):
         for copy in halo_copies(phase)[0]:
@@ -317,24 +328,30 @@
         first = jnp.where((lane >= 61) & (lane < 125), second, pack[: CHANNELS - FOLD])
         zeros = jnp.zeros((8, COLS), F32)
         whole = jnp.concatenate([first, pack[CHANNELS - FOLD : FOLD], zeros], axis=0)
-        pack_send[phase] = whole.astype(BF16)
+        pack_send[phase, 0] = whole.astype(BF16)
         pad = jnp.zeros((MARGIN, PADDED - CHANNELS, COLS), BF16)
         bottom = field[ROWS : ROWS + MARGIN].astype(BF16)
         top = field[MARGIN : 2 * MARGIN].astype(BF16)
         rows_send[phase, 0] = jnp.concatenate([bottom, pad], axis=1)
         rows_send[phase, 1] = jnp.concatenate([top, pad], axis=1)
 
-    def unfold(phase, index):
+    def join_sides(phase):
         lane = iota((112, COLS), 1)
-        from_east = pack_recv[phase, 2 * index].astype(F32)
-        from_west = pack_recv[phase, 2 * index + 1].astype(F32)
-        both = jnp.where(lax.rem(lane, 8) < 4, from_east, from_west)[:FOLD]
-        return jnp.concatenate([both, pltpu.roll(both, 64, 1)], axis=0).astype(BF16)
+        from_east = pack_recv[phase, 0].astype(F32)
+        from_west = pack_recv[phase, 1].astype(F32)
+        both = jnp.where(lax.rem(lane, 8) < 4, from_east, from_west)
+        pack_send[phase, 1] = both.astype(BF16)
+        halo_start_rest(phase, 1)
+        return both
+
+    def unfold(both):
+        first = both[:FOLD]
+        return jnp.concatenate([first, pltpu.roll(first, 64, 1)], axis=0).astype(BF16)
 
     def move_inner(phase, field):
         for row in INNER:
             wide[row, :CHANNELS, :COLS] = field[row].astype(BF16)
-        sides = jnp.dot(unfold(phase, 0), turns[...], preferred_element_type=F32).astype(BF16)
+        sides = jnp.dot(unfold(join_sides(phase)), turns[...], preferred_element_type=F32).astype(BF16)
         for row in range(ROWS):
             wide[MARGIN + row, :, COLS:] = sides[:, row * COLS : (row + 1) * COLS]
         cells = wide[MARGIN : MARGIN + ROWS].reshape(ROWS * PADDED, 2 * COLS)
@@ -347,7 +364,8 @@
             wide[first : first + MARGIN, :, :COLS] = rows
             field[first : first + MARGIN] = rows[:, :CHANNELS].astype(F32)
             turn = turns[:, begin * COLS : (begin + MARGIN) * COLS]
-            sides = jnp.dot(unfold(phase, 1 + index), turn, preferred_element_type=F32)
+            both = pack_recv[phase, 2 + index].astype(F32)
+            sides = jnp.dot(unfold(both), turn, preferred_element_type=F32)
             sides = sides.astype(BF16)
             for row in range(MARGIN):
                 wide[first + row, :, COLS:] = sides[:, row * COLS : (row + 1) * COLS]
@@ -360,14 +378,12 @@
         for phase in range(2):
             rows_recv[phase, 0] = jnp.zeros((MARGIN, PADDED, COLS), BF16)
             pack_recv[phase, 2] = jnp.zeros((112, COLS), BF16)
-            pack_recv[phase, 3] = jnp.zeros((112, COLS), BF16)
 
     @pl.when(jnp.logical_not(has_below))
     def _():
         for phase in range(2):
             rows_recv[phase, 1] = jnp.zeros((MARGIN, PADDED, COLS), BF16)
-            pack_recv[phase, 4] = jnp.zeros((112, COLS), BF16)
-            pack_recv[phase, 5] = jnp.zeros((112, COLS), BF16)
+            pack_recv[phase, 3] = jnp.zeros((112, COLS), BF16)
 
     source = iota((2 * COLS, COLS), 0)
     lane = iota((2 * COLS, COLS), 1)
@@ -394,6 +410,10 @@
         ext[MARGIN + row] = flat[pl.ds(row, CHANNELS, stride=ROWS), :]
     pack_up(0, ext)
 
+    met = 2 + (PLACES - 1) + 2 * (CHIPS - 1) + (LINE - 1) * (DEPTH - 1)
+    pl.semaphore_wait(barrier, met)
+
+    halo_start_sides(0)
     for copy in loads[2:8]:
         copy.wait()
     vectors = [ref[...].astype(F32).reshape(1, CHANNELS) for ref in (bias_v, gain_v, shift_v, dbias_v, scale_v)]
@@ -402,11 +422,7 @@
     for tap in range(TAPS):
         taps[tap] = jnp.broadcast_to(cols[:, tap : tap + 1], (CHANNELS, COLS))
 
-    met = 2 + (PLACES - 1) + (CHIPS - 1)
-    met = met + 2 * has_above.astype(jnp.int32) + 2 * has_below.astype(jnp.int32)
-    pl.semaphore_wait(barrier, met)
-
-    halo_start(0)
+    halo_start_rest(0, 0)
     loads[8].wait()
     flat[...] = (cot_v[...].astype(F32) * mask[None]).reshape(CHANNELS * ROWS, COLS)
     scale_col = cols[:, SCALE : SCALE + 1]
@@ -449,7 +465,7 @@
     gain_col = cols[:, GAIN : GAIN + 1]
     shift_col = cols[:, SHIFT : SHIFT + 1]
 
-    @pl.loop(0, ROWS)
+    @pl.loop(0, ROWS, unroll=ROWS)
     def _(row):
         conv = normed[row]
         offset = conv - jnp.mean(conv, axis=0, keepdims=True)
@@ -461,23 +477,98 @@
         tail = (iota((PADDED - CHANNELS, COLS), 0) == 0).astype(F32).astype(BF16)
         nlow[:, lane_slice(row)] = jnp.concatenate([low, tail], axis=0)
 
-    @pl.loop(0, HIDDEN // CHUNK)
-    def _(chunk):
-        units = pl.ds(pl.multiple_of(chunk * CHUNK, CHUNK), CHUNK)
+    def w_core_copy(part):
+        return remote(
+            w_send.at[part, 1 - core],
+            w_core.at[part],
+            core_ssem.at[part],
+            core_rsem.at[part],
+            g,
+            partner,
+        )
+
+    def w_line_copy(part, k):
+        other = lax.rem((pillar if part == 0 else line) + k, LINE)
+        if part == 0:
+            gg, tt = lax.rem(other, 2) * LINE + line, (depth * 2 + other // 2) * 2 + core
+        else:
+            gg, tt = low * LINE + other, t
+        return remote(
+            w_group.at[part, other],
+            w_group_in.at[part, k],
+            wgroup_ssem.at[part],
+            wgroup_rsem.at[part],
+            gg,
+            tt,
+        )
+
+    def mix(part):
+        units = slice(part * CHUNK, (part + 1) * CHUNK)
         pre = jnp.dot(up_w[units, :], nlow[...], preferred_element_type=F32)
         mass = 0.5 * (1.0 + lax.erf(pre * SQRT_HALF))
         density = GAUSS_SCALE * jnp.exp(-0.5 * pre * pre)
-        act[units, :] = (pre * mass).astype(BF16)
+        active = (pre * mass).astype(BF16)
+        act[units, :] = active
         grad_act = jnp.dot(down_t[units, :], gblow[...], preferred_element_type=F32)
-        gpre[units, :] = (grad_act * (mass + pre * density)).astype(BF16)
+        grad_pre = (grad_act * (mass + pre * density)).astype(BF16)
+        gpre[units, :] = grad_pre
+
+    def weight_grads(part):
+        units = slice(part * CHUNK, (part + 1) * CHUNK)
+        trans = (((1,), (1,)), ((), ()))
+        gup[units, :PADDED] = lax.dot_general(
+            gpre[units, :], nlow[...], trans, preferred_element_type=F32
+        )
+        gdown[units, :CHANNELS] = lax.dot_general(
+            act[units, :], gblow[...], trans, preferred_element_type=F32
+        )
+        for tile in range(part * TILES // 2, (part + 1) * TILES // 2):
+            for half in range(2):
+                begin = tile * SHARE + 16 * half
+                for lanes in range(4):
+                    source = gup if lanes < 2 else gdown
+                    side = (lanes % 2) * COLS
+                    piece = source[begin : begin + 16, side : side + COLS]
+                    if begin + 16 > HIDDEN:
+                        piece = jnp.where(iota((16, COLS), 0) < HIDDEN - begin, piece, 0.0)
+                    along, across, spot = half * 2 + lanes // 2, lanes % 2, tile // 2
+                    if part == 0:
+                        first, second = spot % 2 * 2 + across, along * 4 + spot // 2
+                    else:
+                        first, second = along, across * 8 + spot - 8
+                    w_send[part, tile % 2, first, second] = piece.astype(BF16)
+        w_core_copy(part).start()
+
+    def weight_share(part):
+        finished(w_core_copy(part))
+
+        @pl.loop(0, LINE)
+        def _(piece):
+            total = w_send[part, core, piece].astype(F32) + w_core[part, piece].astype(F32)
+            w_group[part, piece] = total.astype(BF16)
+
+        for k in range(1, LINE):
+            w_line_copy(part, k).start()
+
+    mix(0)
+
+    weight_grads(0)
+
+    mix(1)
+
+    weight_grads(1)
+
+    weight_share(0)
 
     branch[...] = jnp.dot(downw_v[...], act[...], preferred_element_type=F32)
     gnorm[...] = jnp.dot(up_t[...], gpre[...], preferred_element_type=F32)[:CHANNELS]
 
+    weight_share(1)
+
     sums[...] = jnp.zeros_like(sums)
     down_bias = cols[:, DOWN_BIAS : DOWN_BIAS + 1]
 
-    @pl.loop(0, ROWS)
+    @pl.loop(0, ROWS, unroll=4)
     def _(row):
         grad = gnorm[:, lane_slice(row)]
         unit = normed[row]
@@ -494,29 +585,8 @@
         sums[0] += low
 
     pack_up(1, exg)
-    halo_start(1)
-
-    trans = (((1,), (1,)), ((), ()))
-    gup[:HIDDEN, :PADDED] = lax.dot_general(gpre[...], nlow[...], trans, preferred_element_type=F32)
-    gdown[:HIDDEN, :CHANNELS] = lax.dot_general(
-        act[...], gblow[...], trans, preferred_element_type=F32
-    )
-
-    for tile in range(TILES):
-        for half in range(2):
-            begin = tile * SHARE + 16 * half
-            for part in range(4):
-                source = gup if part < 2 else gdown
-                side = (part % 2) * COLS
-                piece = source[begin : begin + 16, side : side + COLS]
-                if begin + 16 > HIDDEN:
-                    piece = jnp.where(iota((16, COLS), 0) < HIDDEN - begin, piece, 0.0)
-                w_send[tile % 2, half * 4 + part, tile // 2] = piece.astype(BF16)
-
-    w_core_copy = remote(
-        w_send.at[1 - core], w_core, core_ssem.at[0], core_rsem.at[0], g, partner
-    )
-    w_core_copy.start()
+    halo_start_sides(1)
+    halo_start_rest(1, 0)
 
     def tap_block(block):
         rows = block_rows(block)
@@ -536,25 +606,7 @@
             out = jnp.where(lane == TAPS + vector, total, out)
         small_wide[rows, :] = out * live
 
-    pl.loop(0, 10, unroll=UNROLL)(tap_block)
-
-    finished(w_core_copy)
-
-    @pl.loop(0, GROUPS)
-    def _(piece):
-        total = w_send[core, piece].astype(F32) + w_core[piece].astype(F32)
-        w_group[piece] = total.astype(BF16)
-
-    def w_group_copy(k):
-        other = lax.rem(g + k, GROUPS)
-        return remote(
-            w_group.at[other], w_group_in.at[k], wgroup_ssem.at[k], wgroup_rsem.at[k], other, t
-        )
-
-    for k in range(1, GROUPS):
-        w_group_copy(k).start()
-
-    pl.loop(10, BLOCKS, unroll=UNROLL)(tap_block)
+    pl.loop(0, BLOCKS, unroll=UNROLL)(tap_block)
 
     second = pltpu.roll(small_wide[FOLD:], 64, 1)
     whole = jnp.concatenate(
@@ -569,7 +621,7 @@
 
     def s_copy(k):
         gg, tt, other = other_place(k)
-        return remote(small.at[other], small_in.at[k], small_ssem.at[k], small_rsem.at[k], gg, tt)
+        return remote(small.at[other], small_in.at[k], small_ssem, small_rsem, gg, tt)
 
     for k in range(1, PLACES):
         s_copy(k).start()
@@ -593,67 +645,92 @@
             spots = pl.ds(block * 64 + row, 8, stride=ROWS)
             flat[spots, :] = cell * (mgrad[row, rows, :] + total[row])
 
-    pl.loop(0, 10, unroll=UNROLL)(finish_inner)
-
-    total = w_group[g].astype(F32)
-    for k in range(1, GROUPS):
-        finished(w_group_copy(k))
-        total = total + w_group_in[k].astype(F32)
-    w_tile[...] = total.astype(BF16)
-
-    def w_tile_copy(k):
-        other = lax.rem(chip + k, CHIPS)
+    pl.loop(0, 15, unroll=UNROLL)(finish_inner)
+
+    for part in range(2):
+        total = w_group[part, pillar if part == 0 else line].astype(F32)
+        all_finished(w_group_in.at[part], LINE - 1, wgroup_ssem.at[part], wgroup_rsem.at[part])
+        for k in range(1, LINE):
+            total = total + w_group_in[part, k].astype(F32)
+        w_tile[part] = total.astype(BF16)
+
+    near = line * 4 + lax.rem(depth, 4)
+    far = low * 8 + lax.rem(chip, 8)
+
+    def w_tile_copy(part, k):
+        if part == 0:
+            other = lax.rem(near + k, 16)
+            gg, tt = low * LINE + other // 4, (lax.rem(other, 4) * 2 + high) * 2 + core
+        else:
+            other = lax.rem(far + k, 16)
+            gg, tt = other // 8 * LINE + line, (8 + lax.rem(other, 8)) * 2 + core
         return remote(
-            w_tile.at[other],
-            w_tile_in.at[chip],
-            wtile_ssem.at[k],
-            wtile_rsem.at[k],
-            g,
-            other * 2 + core,
+            w_tile.at[part, other],
+            w_tile_in.at[sheet if part == 0 else plane],
+            wtile_ssem,
+            wtile_rsem,
+            gg,
+            tt,
         )
 
-    for k in range(1, CHIPS):
-        w_tile_copy(k).start()
+    for k in range(1, 16):
+        w_tile_copy(0, k).start()
+        w_tile_copy(1, k).start()
+
+    @pl.when(upper == 1)
+    def _():
+        w_tile_copy(0, 0).start()
+
+    @pl.when(upper == 0)
+    def _():
+        w_tile_copy(1, 0).start()
 
     total = small[place]
+    all_finished(small_in, PLACES - 1, small_ssem, small_rsem)
     for k in range(1, PLACES):
-        finished(s_copy(k))
         total = total + small_in[k]
     s_tile[...] = total
 
     def s_tile_copy(k):
         other = lax.rem(chip + k, CHIPS)
         return remote(
-            s_tile, s_tile_in.at[chip], stile_ssem.at[k], stile_rsem.at[k], g, other * 2 + core
+            s_tile, s_tile_in.at[chip], stile_ssem, stile_rsem, g, other * 2 + core
         )
 
     for k in range(1, CHIPS):
         s_tile_copy(k).start()
 
-    pl.loop(10, BLOCKS, unroll=UNROLL)(finish_inner)
+    pl.loop(15, BLOCKS, unroll=UNROLL)(finish_inner)
 
     halo_wait_rest(1)
 
     move_outer(1, exg)
 
-    w_tile_in[chip] = w_tile[chip]
-    for k in range(1, CHIPS):
-        finished(w_tile_copy(k))
+    pl.loop(0, BLOCKS, unroll=UNROLL)(finish_outer)
+
+    state_v[...] = flat[...].reshape(CHANNELS, ROWS, COLS).astype(BF16)
+    store = pltpu.make_async_copy(state_v, gs_ref, store_sem)
+    store.start()
+
+    w_tile_in[upper * plane + (1 - upper) * sheet] = w_tile[upper, upper * far + (1 - upper) * near]
+    all_finished(w_tile_in, PLANE - 1, wtile_ssem, wtile_rsem)
     total = w_tile_in[0].astype(F32)
-    for other in range(1, CHIPS):
+    for other in range(1, PLANE):
         total = total + w_tile_in[other].astype(F32)
-    w_final[g] = total
+    piece = line * 2 + low
+    w_final[piece] = total
 
     def w_final_copy(k):
         other = lax.rem(g + k, GROUPS)
-        return remote(w_final.at[g], w_final.at[g], wfinal_ssem.at[k], wfinal_rsem.at[k], other, t)
+        return remote(
+            w_final.at[piece], w_final.at[piece], wfinal_ssem, wfinal_rsem, other, t
+        )
 
     for k in range(1, GROUPS):
         w_final_copy(k).start()
 
     s_tile_in[chip] = s_tile[...]
-    for k in range(1, CHIPS):
-        finished(s_tile_copy(k))
+    all_finished(s_tile_in, CHIPS - 1, stile_ssem, stile_rsem)
     total = s_tile_in[0]
     for other in range(1, CHIPS):
         total = total + s_tile_in[other]
@@ -662,22 +739,14 @@
     def s_final_copy(k):
         gg, tt, _ = other_place(k)
         return remote(
-            s_final.at[place], s_final.at[place], sfinal_ssem.at[k], sfinal_rsem.at[k], gg, tt
+            s_final.at[place], s_final.at[place], sfinal_ssem, sfinal_rsem, gg, tt
         )
 
     for k in range(1, PLACES):
         s_final_copy(k).start()
 
-    pl.loop(0, BLOCKS, unroll=UNROLL)(finish_outer)
-
-    state_v[...] = flat[...].reshape(CHANNELS, ROWS, COLS).astype(BF16)
-    store = pltpu.make_async_copy(state_v, gs_ref, store_sem)
-    store.start()
-
-    for k in range(1, GROUPS):
-        finished(w_final_copy(k))
-    for k in range(1, PLACES):
-        finished(s_final_copy(k))
+    all_finished(w_final, GROUPS - 1, wfinal_ssem, wfinal_rsem)
+    all_finished(s_final, PLACES - 1, sfinal_ssem, sfinal_rsem)
     factor = 1.0 / math.sqrt(CELLS * GROUPS * TILES)
     tail_ref[0] = w_final[...].reshape(128, COLS) * factor
     tail_ref[1] = s_final[...].reshape(128, COLS) * factor
@@ -689,7 +758,7 @@
     tile = (CHANNELS, ROWS, COLS)
     rows = (ROWS, CHANNELS, COLS)
     tall = (TALL, CHANNELS, COLS)
-    pieces = (GROUPS, CHIPS, 16, COLS)
+    pieces = (LINE, 16, 16, COLS)
     return [
         pltpu.VMEM((ROWS, COLS), jnp.int32),
         pltpu.VMEM(tile, BF16),
@@ -731,14 +800,14 @@
         pltpu.VMEM(rows, F32),
         pltpu.VMEM((2, 2, MARGIN, PADDED, COLS), BF16),
         pltpu.VMEM((2, 2, MARGIN, PADDED, COLS), BF16),
-        pltpu.VMEM((2, 112, COLS), BF16),
-        pltpu.VMEM((2, 6, 112, COLS), BF16),
+        pltpu.VMEM((2, 2, 112, COLS), BF16),
+        pltpu.VMEM((2, 4, 112, COLS), BF16),
+        pltpu.VMEM((2, 2) + pieces, BF16),
         pltpu.VMEM((2,) + pieces, BF16),
-        pltpu.VMEM(pieces, BF16),
-        pltpu.VMEM(pieces, BF16),
-        pltpu.VMEM(pieces, BF16),
-        pltpu.VMEM((CHIPS, 16, COLS), BF16),
-        pltpu.VMEM((CHIPS, 16, COLS), BF16),
+        pltpu.VMEM((2,) + pieces, BF16),
+        pltpu.VMEM((2,) + pieces, BF16),
+        pltpu.VMEM((2, 16, 16, COLS), BF16),
+        pltpu.VMEM((PLANE, 16, COLS), BF16),
         pltpu.VMEM((GROUPS, 16, COLS), F32),
         pltpu.VMEM((PLACES, 8, COLS), F32),
         pltpu.VMEM((PLACES, 8, COLS), F32),
@@ -747,30 +816,28 @@
         pltpu.VMEM((PLACES, 8, COLS), F32),
         dma((12,)),
         dma(()),
-        dma((2, 8)),
-        dma((2, 8)),
-        dma((1,)),
-        dma((1,)),
-        dma((GROUPS,)),
-        dma((GROUPS,)),
-        dma((PLACES,)),
-        dma((PLACES,)),
-        dma((CHIPS,)),
-        dma((CHIPS,)),
-        dma((CHIPS,)),
-        dma((CHIPS,)),
-        dma((GROUPS,)),
-        dma((GROUPS,)),
-        dma((PLACES,)),
-        dma((PLACES,)),
+        dma((2, 6)),
+        dma((2, 6)),
+        dma((2,)),
+        dma((2,)),
+        dma((2,)),
+        dma((2,)),
+        dma(()),
+        dma(()),
+        dma(()),
+        dma(()),
+        dma(()),
+        dma(()),
+        dma(()),
+        dma(()),
+        dma(()),
+        dma(()),
     ]
 
 
-def place_results(
-    rows_ref, tail_ref, gs_ref, up_ref, ubias_ref, down_ref, taps_ref, vec_ref, rows, sems
-):
-    load = pltpu.make_async_copy(rows_ref, rows, sems.at[0])
-    load.start()
+def place_results(rows_ref, tail_ref, gs_ref, up_ref, ubias_ref, down_ref, taps_ref, vec_ref, sem):
+    copy = pltpu.make_async_copy(rows_ref, gs_ref, sem)
+    copy.start()
     for half, size in ((0, 16), (1, SHARE - 16)):
         for part in range(4):
             piece = tail_ref[0, (half * 4 + part) * 16 : (half * 4 + part) * 16 + size, :]
@@ -778,9 +845,6 @@
             begin = (part % 2) * COLS
             width = min(COLS, CHANNELS - begin)
             target[half * 16 : half * 16 + size, begin : begin + width] = piece[:, :width]
-    load.wait()
-    copy = pltpu.make_async_copy(rows, gs_ref, sems.at[1])
-    copy.start()
     edge = jnp.concatenate([tail_ref[0, 16:32, :], tail_ref[0, 80:96, :]], axis=0)
     line = edge.T[CHANNELS - COLS : CHANNELS - COLS + 1, :SHARE]
     ubias_ref[...] = line.reshape(SHARE)
@@ -846,9 +910,9 @@
             jax.ShapeDtypeStruct((TAPS, CHANNELS), F32),
             jax.ShapeDtypeStruct((5, CHANNELS), F32),
         ),
-        in_specs=[anywhere, vmem],
+        in_specs=[vmem, vmem],
         out_specs=(anywhere,) + (vmem,) * 5,
-        scratch_shapes=[pltpu.VMEM((CHANNELS, ROWS, COLS), BF16), pltpu.SemaphoreType.DMA((2,))],
+        scratch_shapes=[pltpu.SemaphoreType.DMA(())],
     )(grad_rows, tail)
     return grad_state[None], grad_up, grad_up_bias, grad_down.T, grad_taps.T, grad_vectors
 

time: 61.4 us -> 52.3 us (0.85)
  Pallas kernels: 59.8 us -> 50.7 us
    pallas_call x1, Pallas kernels: 56.4 us -> 48.3 us  [local(): pl.pallas_call(kernel, out_shape=(jax.ShapeDtypeStruct((CHANNELS, ROWS, C...]
    pallas_call x1, Pallas kernels: 3.32 us -> 2.44 us  [local(): pl.pallas_call(place_results, out_shape=(jax.ShapeDtypeStruct((CHANNELS,...]
where the time goes in v3:
time: 52.3 us; the launch traced here: 52.2 us
  Pallas kernels  50.7 us (97%)
  between operations  1.45 us (3%)
    pallas_call x1, Pallas kernels, local(): pl.pallas_call(kernel, out_shape=(jax.ShapeDtypeStruct((CHANNELS, ROWS, C...  48.3 us
    pallas_call x1, Pallas kernels, local(): pl.pallas_call(place_results, out_shape=(jax.ShapeDtypeStruct((CHANNELS,...  2.44 us

profile of v3, /device:TPU:1, one launch (start us, length us, event | category | flops | bytes accessed | tf_op | source)
XLA Modules:
  0.0 52.2 jit_solution(7156013731214023463)
XLA Ops:
  1.3 48.3 %shard_map.172 = (bf16[200,8,128]{2,1,0:T(8,128)(2,1)}, f32[2,128,128]{2,1,0:T(8,128)}) custom-call(s32[1]{0:T(128)S(6)} %copy.19.slot_ref, s32[8,128]{1,0:T(8,128)} %bitcast.12, bf16[200,8,128]{2,1,0:T(8,128)(2,1)} %bitcast.8, bf16[200,8,128]{2,1,0:T(8,128)(2,1)} %bitcast.9, bf16[49,200]{1,0:T(8,128)(2,1)} %bitcast.11, bf16[200,800]{1,0:T(8,128)(2,1)} %bitcast.10, ...), custom_call_target="tpu_custom_call" | custom-call | tf_op jit(solution)/shard_map/pallas_call | solution.py:876
  49.6 2.4 %shard_map.173 = (bf16[200,8,128]{2,1,0:T(8,128)(2,1)}, f32[25,200]{1,0:T(8,128)}, f32[25]{0:T(128)}, f32[25,200]{1,0:T(8,128)}, f32[49,200]{1,0:T(8,128)}, /*index=5*/f32[5,200]{1,0:T(8,128)}) custom-call(bf16[200,8,128]{2,1,0:T(8,128)(2,1)} %get-tuple-element.14.rows_ref, f32[2,128,128]{2,1,0:T(8,128)} %get-tuple-element.15.tail_ref), custom_call_target="tpu_custom_call" | custom-call | tf_op jit(solution)/shard_map/pallas_call | solution.py:903

commit v4 on v3

--- a/solution.py
+++ b/solution.py
@@ -348,9 +348,11 @@
         first = both[:FOLD]
         return jnp.concatenate([first, pltpu.roll(first, 64, 1)], axis=0).astype(BF16)
 
-    def move_inner(phase, field):
+    def fill_inner(field):
         for row in INNER:
             wide[row, :CHANNELS, :COLS] = field[row].astype(BF16)
+
+    def move_inner(phase):
         sides = jnp.dot(unfold(join_sides(phase)), turns[...], preferred_element_type=F32).astype(BF16)
         for row in range(ROWS):
             wide[MARGIN + row, :, COLS:] = sides[:, row * COLS : (row + 1) * COLS]
@@ -438,9 +440,10 @@
     up_w[...] = up_t[...].T
     down_t[...] = downw_v[...].T
 
+    fill_inner(ext)
     halo_wait_sides(0)
 
-    move_inner(0, ext)
+    move_inner(0)
 
     @pl.loop(0, BLOCKS, unroll=UNROLL)
     def _(block):
@@ -556,14 +559,10 @@
 
     mix(1)
 
-    weight_grads(1)
-
     weight_share(0)
 
     branch[...] = jnp.dot(downw_v[...], act[...], preferred_element_type=F32)
     gnorm[...] = jnp.dot(up_t[...], gpre[...], preferred_element_type=F32)[:CHANNELS]
-
-    weight_share(1)
 
     sums[...] = jnp.zeros_like(sums)
     down_bias = cols[:, DOWN_BIAS : DOWN_BIAS + 1]
@@ -586,6 +585,8 @@
 
     pack_up(1, exg)
     halo_start_sides(1)
+
+    weight_grads(1)
     halo_start_rest(1, 0)
 
     def tap_block(block):
@@ -626,9 +627,12 @@
     for k in range(1, PLACES):
         s_copy(k).start()
 
+    weight_share(1)
+
+    fill_inner(exg)
     halo_wait_sides(1)
 
-    move_inner(1, exg)
+    move_inner(1)
 
     def finish_inner(block):
         rows = block_rows(block)
@@ -644,15 +648,6 @@
             cell = mask[row : row + 1]
             spots = pl.ds(block * 64 + row, 8, stride=ROWS)
             flat[spots, :] = cell * (mgrad[row, rows, :] + total[row])
-
-    pl.loop(0, 15, unroll=UNROLL)(finish_inner)
-
-    for part in range(2):
-        total = w_group[part, pillar if part == 0 else line].astype(F32)
-        all_finished(w_group_in.at[part], LINE - 1, wgroup_ssem.at[part], wgroup_rsem.at[part])
-        for k in range(1, LINE):
-            total = total + w_group_in[part, k].astype(F32)
-        w_tile[part] = total.astype(BF16)
 
     near = line * 4 + lax.rem(depth, 4)
     far = low * 8 + lax.rem(chip, 8)
@@ -673,17 +668,23 @@
             tt,
         )
 
-    for k in range(1, 16):
-        w_tile_copy(0, k).start()
-        w_tile_copy(1, k).start()
-
-    @pl.when(upper == 1)
-    def _():
-        w_tile_copy(0, 0).start()
-
-    @pl.when(upper == 0)
-    def _():
-        w_tile_copy(1, 0).start()
+    def w_piece_sums(part):
+        total = w_group[part, pillar if part == 0 else line].astype(F32)
+        all_finished(w_group_in.at[part], LINE - 1, wgroup_ssem.at[part], wgroup_rsem.at[part])
+        for k in range(1, LINE):
+            total = total + w_group_in[part, k].astype(F32)
+        w_tile[part] = total.astype(BF16)
+
+        @pl.when(upper != part)
+        def _():
+            w_tile_copy(part, 0).start()
+
+        for k in range(1, 16):
+            w_tile_copy(part, k).start()
+
+    pl.loop(0, 15, unroll=UNROLL)(finish_inner)
+
+    w_piece_sums(0)
 
     total = small[place]
     all_finished(small_in, PLACES - 1, small_ssem, small_rsem)
@@ -701,6 +702,8 @@
         s_tile_copy(k).start()
 
     pl.loop(15, BLOCKS, unroll=UNROLL)(finish_inner)
+
+    w_piece_sums(1)
 
     halo_wait_rest(1)
 

time: 52.3 us -> 52 us (level)
  no operation moved by 1% of the time
where the time goes in v4:
time: 52 us; the launch traced here: 51.8 us
  Pallas kernels  50.4 us (97%)
  between operations  1.45 us (3%)
    pallas_call x1, Pallas kernels, local(): pl.pallas_call(kernel, out_shape=(jax.ShapeDtypeStruct((CHANNELS, ROWS, C...  47.9 us
    pallas_call x1, Pallas kernels, local(): pl.pallas_call(place_results, out_shape=(jax.ShapeDtypeStruct((CHANNELS,...  2.44 us

profile of v4, /device:TPU:1, one launch (start us, length us, event | category | flops | bytes accessed | tf_op | source)
XLA Modules:
  0.0 51.8 jit_solution(12378631398638505481)
XLA Ops:
  1.3 47.9 %shard_map.172 = (bf16[200,8,128]{2,1,0:T(8,128)(2,1)}, f32[2,128,128]{2,1,0:T(8,128)}) custom-call(s32[1]{0:T(128)S(6)} %copy.19.slot_ref, s32[8,128]{1,0:T(8,128)} %bitcast.12, bf16[200,8,128]{2,1,0:T(8,128)(2,1)} %bitcast.8, bf16[200,8,128]{2,1,0:T(8,128)(2,1)} %bitcast.9, bf16[49,200]{1,0:T(8,128)(2,1)} %bitcast.11, bf16[200,800]{1,0:T(8,128)(2,1)} %bitcast.10, ...), custom_call_target="tpu_custom_call" | custom-call | tf_op jit(solution)/shard_map/pallas_call | solution.py:879
  49.2 2.4 %shard_map.173 = (bf16[200,8,128]{2,1,0:T(8,128)(2,1)}, f32[25,200]{1,0:T(8,128)}, f32[25]{0:T(128)}, f32[25,200]{1,0:T(8,128)}, f32[49,200]{1,0:T(8,128)}, /*index=5*/f32[5,200]{1,0:T(8,128)}) custom-call(bf16[200,8,128]{2,1,0:T(8,128)(2,1)} %get-tuple-element.14.rows_ref, f32[2,128,128]{2,1,0:T(8,128)} %get-tuple-element.15.tail_ref), custom_call_target="tpu_custom_call" | custom-call | tf_op jit(solution)/shard_map/pallas_call | solution.py:906
